TPU v7x, 256 devices: a whole 4x4x8 slice. The times are simulated.
256 devices in a mesh: gx: 16 (over z, x_lo), gy: 16 (over x_hi, y, core).
Axes of the slice: x: 4 (x_hi: 2, x_lo: 2; x = x_hi * 2 + x_lo), y: 4, z: 8, core: 2. Of those that a mesh axis runs over, the one named last changes fastest.
Arguments:
- volume: float32 [64, 2048, 2048], P(None, 'gy', 'gx'), may hold values from -6 to 6
Outputs:
- derivatives: float32 [9, 64, 256, 256], P(None, 'gx', 'gy')
All inputs are finite; a program needn't handle non-finite values.
Results may differ from a plain program's by a relative error of at most 0.00011.
Values sent between devices are 32-bit elements; how exact they have to be, the bound alone decides.
No kernel may reach another device: no remote copies, remote signals or barrier semaphores. Data moves between devices by JAX's collectives and lax.ppermute only.
A program may use at most 128 MiB of HBM per device.

v0:
```python
import math

import jax
import jax.numpy as jnp
import ml_dtypes
import numpy as np
from jax import lax
from jax.experimental import pallas as pl
from jax.experimental.pallas import tpu as pltpu
from jax.sharding import PartitionSpec as P

NX = 2048
NY = 2048
NZ = 64
MX = 256
MY = 256
GROUP = 16
VMEM_LIMIT = 24 * 1024 * 1024
F32 = jnp.float32
BF16 = jnp.bfloat16


def basis_order(modes):
    k = (np.arange(modes) + 1) // 2
    return np.argsort(k % 2, kind="stable")


def forward_table(points, modes):
    k = np.arange(1, modes // 2)[:, None]
    angle = 2.0 * math.pi * ((k * np.arange(points)[None, :]) % points) / points
    table = np.zeros((modes, points))
    table[0] = 1.0
    table[1:-1:2] = np.cos(angle)
    table[2:-1:2] = np.sin(angle)
    return table[basis_order(modes)]


def folded_table(points, modes):
    return forward_table(points, modes)[:, : points // 2].reshape(2, modes // 2, points // 2)


def inverse_table(points, modes, power):
    k = np.arange(1, modes // 2)[None, :]
    angle = 2.0 * math.pi * ((k * np.arange(modes)[:, None]) % modes) / modes
    fine = 2.0 * math.pi * k / points
    weight = 2.0 * np.exp(-0.5 * fine * fine) * (2.0 * math.pi * k / modes) ** power / points
    on_cos, on_sin = [
        (np.cos(angle), np.sin(angle)),
        (-np.sin(angle), np.cos(angle)),
        (-np.cos(angle), -np.sin(angle)),
    ][power]
    table = np.zeros((modes, modes))
    table[:, 0] = 1.0 / points if power == 0 else 0.0
    table[:, 1:-1:2] = weight * on_cos
    table[:, 2:-1:2] = weight * on_sin
    return table[:, basis_order(modes)]


def circulant_table(points, power):
    return inverse_table(points, points, power) @ forward_table(points, points)


def split(table, axis=None):
    table = np.asarray(table, np.float32)
    high = table.astype(ml_dtypes.bfloat16)
    rest = table - high.astype(np.float32)
    if axis is None:
        return high, rest.astype(ml_dtypes.bfloat16)
    rest = np.moveaxis(rest, axis, 0)
    low = np.zeros(rest.shape, ml_dtypes.bfloat16)
    carry = np.zeros(rest.shape[1:], np.float32)
    for n in range(rest.shape[0]):
        wanted = rest[n] + carry
        low[n] = wanted.astype(ml_dtypes.bfloat16)
        carry = wanted - low[n].astype(np.float32)
    return high, np.moveaxis(low, 0, axis)


def z_table():
    ops = np.stack([circulant_table(NZ, power) for power in range(3)])
    ops = ops.reshape(3, GROUP, NZ // GROUP, NZ).transpose(1, 0, 2, 3).reshape(3 * NZ, NZ)
    return [np.kron(part, np.eye(2, dtype=ml_dtypes.bfloat16)) for part in split(ops, 1)]


def y_table():
    ops = np.concatenate([inverse_table(NY, MY, power) for power in range(3)])
    ops = ops.reshape(3 * MY, GROUP, 2, 8).transpose(0, 3, 2, 1)
    return ops.reshape(3 * MY, MY)


def split_value(value):
    high = value.astype(BF16)
    return high, (value - high.astype(F32)).astype(BF16)


def dot(a, b):
    return jnp.dot(a, b, preferred_element_type=F32)


def dot3(a, b):
    return dot(a[0], b[0]) + dot(a[0], b[1]) + dot(a[1], b[0])


def swap_blocks(arrays):
    block = lax.broadcasted_iota(jnp.int32, arrays[0].shape, 1) // 16
    arrays = list(arrays)
    for step in (1, 2, 4):
        upper = (block & step) != 0
        swapped = list(arrays)
        for a in range(8):
            if a & step == 0:
                first, second = arrays[a], arrays[a | step]
                swapped[a] = jnp.where(upper, pltpu.roll(second, 16 * step, 1), first)
                swapped[a | step] = jnp.where(upper, second, pltpu.roll(first, 128 - 16 * step, 1))
        arrays = swapped
    return arrays


def fold(first, second):
    return split_value(first + second), split_value(first - second)


def forward_y(v_ref, high_ref, low_ref, out_ref):
    planes = v_ref.shape[1]
    ends = [
        jnp.concatenate([v_ref[8 * e : 8 * e + 8, z].reshape(NY // 2, 128) for z in range(planes)], axis=1)
        for e in range(2)
    ]
    for parity, lines in enumerate(fold(*ends)):
        product = dot3((high_ref[parity], low_ref[parity]), lines)
        for z in range(planes):
            piece = product[:, 128 * z : 128 * (z + 1)].reshape(GROUP // 2, GROUP, 128)
            out_ref[8 * parity : 8 * parity + 8, z] = piece


def forward_x(v_ref, high_ref, low_ref, out_ref, total):
    rows = v_ref.shape[1]
    ends = [jnp.concatenate([v_ref[8 * e + s] for s in range(8)], axis=1) for e in range(2)]
    for parity, (high, low) in enumerate(fold(*ends)):
        both = dot(jnp.concatenate([high, low], axis=0), high_ref[parity])
        total[parity] = both[:rows] + both[rows:] + dot(high, low_ref[parity])
        lines = [total[parity, pl.ds(q, 8, stride=8), :] for q in range(8)]
        for k, message in enumerate(swap_blocks(lines)):
            out_ref[8 * parity + k] = message


def along_z(v_ref, high_ref, low_ref, out_ref):
    out_ref[...] = dot3((high_ref[...], low_ref[...]), split_value(v_ref[...]))


def inverse_y(v_ref, high_ref, low_ref, out_ref):
    def lines(power, z, half):
        return v_ref[pl.ds(8 * power + 2 * z + half, GROUP, stride=24), :]

    columns = []
    for second in (1, 2):
        halves = [
            swap_blocks([lines(power, z, half) for power in (0, second) for z in range(4)])
            for half in range(2)
        ]
        columns.append(
            jnp.concatenate([halves[half][low] for low in range(8) for half in range(2)], axis=0)
        )
    product = dot3((high_ref[...], low_ref[...]), split_value(jnp.concatenate(columns, axis=1)))
    lane = lax.broadcasted_iota(jnp.int32, (MY, 128), 1)
    pieces = (
        product[:MY, :128],
        product[MY : 2 * MY, :128],
        jnp.where(lane < 64, product[2 * MY :, 128:], product[:MY, 128:]),
    )
    for k, piece in enumerate(pieces):
        out_ref[:, k] = piece.reshape(GROUP, GROUP, 128)


PLACES = {(0, 0): 0, (0, 1): 1, (1, 0): 2, (1, 1): 3, (2, 0): 4, (0, 2): 5}
FIELDS = (
    ((1, (1, 0)), (2, (0, 1)), (4, (2, 0)), (5, (0, 2)), (8, (1, 1))),
    ((0, (0, 0)), (6, (1, 0)), (7, (0, 1))),
    ((3, (0, 0)),),
)


def inverse_x(v_ref, high_ref, low_ref, out_ref, held, sems):
    combos, copies = [], []
    for k in range(3):
        halves = [swap_blocks([v_ref[8 * half + s, k] for s in range(8)]) for half in range(2)]
        for part in range(2):
            rows = [
                jnp.concatenate([halves[0][4 * part + z], halves[1][4 * part + z]], axis=1)
                for z in range(4)
            ]
            combos.append(jnp.concatenate(rows, axis=0))
    for power in (2, 1, 0):
        table = (
            high_ref[:, MX * power : MX * (power + 1)],
            low_ref[:, MX * power : MX * (power + 1)],
        )
        lines = jnp.concatenate([combos[PLACES[yz]] for _, yz in FIELDS[power]], axis=0)
        product = dot3(split_value(lines), table)
        for n, (field, _) in enumerate(FIELDS[power]):
            for z in range(4):
                start = 64 * n + 16 * z
                held[field, z] = product[start : start + 16]
            copies.append(pltpu.make_async_copy(held.at[field], out_ref.at[field], sems.at[field]))
            copies[-1].start()
    for copy in copies:
        copy.wait()


WHOLE = pl.BlockSpec(memory_space=pltpu.VMEM)


def call(kernel, out_shape, operands, out_specs=WHOLE, scratch=()):
    return pl.pallas_call(
        kernel,
        out_shape=jax.ShapeDtypeStruct(out_shape, F32),
        in_specs=[WHOLE] * len(operands),
        out_specs=out_specs,
        scratch_shapes=list(scratch),
        compiler_params=pltpu.CompilerParams(vmem_limit_bytes=VMEM_LIMIT),
    )(*operands)


def exchange(value, axis):
    return lax.all_to_all(value, axis, split_axis=0, concat_axis=0, tiled=True)


def on_device(volume):
    y_high, y_low = split(folded_table(NY, MY), 2)
    x_high, x_low = split(folded_table(NX, MX).transpose(0, 2, 1), 1)
    lines = exchange(volume.reshape(GROUP, 4 * 128, 128), "gy").reshape(GROUP, 4, 128, 128)
    lines = call(
        forward_y,
        (GROUP, 4, GROUP, 128),
        (lines, y_high, y_low),
    )

    lines = exchange(lines.reshape(GROUP, 64, 128), "gx")
    lines = call(
        forward_x,
        (GROUP, 8, 128),
        (lines, x_high, x_low),
        scratch=(pltpu.VMEM((2, 64, 128), F32),),
    )

    lines = exchange(lines, "gy").reshape(GROUP * 8, 128)
    lines = call(along_z, (6 * NZ, 128), (lines, *z_table()))

    lines = exchange(lines.reshape(GROUP, 24, 128), "gx").reshape(6 * NZ, 128)
    lines = call(inverse_y, (GROUP, 3, GROUP, 128), (lines, *split(y_table())))

    lines = exchange(lines.reshape(GROUP, 48, 128), "gy").reshape(GROUP, 3, GROUP, 128)
    back_x = np.concatenate([inverse_table(NX, MX, power).T for power in range(3)], axis=1)
    return call(
        inverse_x,
        (9, 4, GROUP, MX),
        (lines, *split(back_x)),
        out_specs=pl.BlockSpec(memory_space=pl.ANY),
        scratch=(pltpu.VMEM((9, 4, GROUP, MX), F32), pltpu.SemaphoreType.DMA((9,))),
    )


def solution(mesh):
    return jax.shard_map(
        on_device,
        mesh=mesh,
        in_specs=(P(None, "gy", "gx"),),
        out_specs=P(None, "gx", "gy", None),
        check_vma=False,
    )
```

profile of v0, /device:TPU:1, one launch (start us, length us, event | category | flops | bytes accessed | tf_op | source)
XLA Modules:
  0.0 128.6 jit_solution(6050226798408074392)
XLA Ops:
  0.0 0.0 copy-start.2
  0.0 0.0 copy-start.3
  0.0 59.2 %all_to_all.25 = f32[16,512,128]{2,1,0:T(8,128)S(1)} all-to-all(f32[16,512,128]{2,1,0:T(8,128)} %bitcast.15), channel_id=1, replica_groups=mesh['gx'=16,'gy'=16] {'gy'}, dimensions={0} | all-to-all | bytes 8388608 | tf_op jit(solution)/shard_map/all_to_all | solution.py:225
  59.2 0.0 copy-start
  59.2 0.0 copy-start.1
  59.2 0.0 copy-done.2
  59.2 0.0 copy-done.3
  59.2 0.0 copy-start.8
  59.2 0.0 copy-start.9
  59.2 0.0 copy-start.6
  59.2 0.0 copy-start.7
  59.3 1.3 %shard_map.109 = f32[16,4,16,128]{3,2,1,0:T(8,128)S(1)} custom-call(f32[16,4,128,128]{3,2,1,0:T(8,128)S(1)} %bitcast.8, bf16[2,128,1024]{2,1,0:T(8,128)(2,1)S(1)} %copy-done.3, bf16[2,128,1024]{2,1,0:T(8,128)(2,1)S(1)} %copy-done.2), custom_call_target="tpu_custom_call" | custom-call | tf_op jit(solution)/shard_map/pallas_call | solution.py:214
  60.6 0.0 copy-start.4
  60.6 0.0 copy-start.5
  60.6 23.7 %all_to_all.26.v_ref = f32[16,64,128]{2,1,0:T(8,128)S(1)} all-to-all(f32[16,64,128]{2,1,0:T(8,128)S(1)} %bitcast.9), channel_id=1, replica_groups=mesh['gx'=16,'gy'=16] {'gx'}, dimensions={0} | all-to-all | bytes 1048576 | tf_op jit(solution)/shard_map/all_to_all | solution.py:225
  84.3 0.0 copy-done
  84.3 0.0 copy-done.1
  84.3 0.6 shard_map.110
  84.9 14.3 %all_to_all.27 = f32[16,8,128]{2,1,0:T(8,128)S(1)} all-to-all(f32[16,8,128]{2,1,0:T(8,128)S(1)} %shard_map.110), channel_id=1, replica_groups=mesh['gx'=16,'gy'=16] {'gy'}, dimensions={0} | all-to-all | bytes 131072 | tf_op jit(solution)/shard_map/all_to_all | solution.py:225
  99.2 0.0 copy-done.8
  99.2 0.0 copy-done.9
  99.2 0.2 shard_map.111
  99.4 12.5 %all_to_all.28 = f32[16,24,128]{2,1,0:T(8,128)S(1)} all-to-all(f32[16,24,128]{2,1,0:T(8,128)S(1)} %bitcast.12), channel_id=1, replica_groups=mesh['gx'=16,'gy'=16] {'gx'}, dimensions={0} | all-to-all | bytes 393216 | tf_op jit(solution)/shard_map/all_to_all | solution.py:225
  111.9 0.0 copy-done.6
  111.9 0.0 copy-done.7
  111.9 0.7 shard_map.112
  112.6 14.6 %all_to_all.29 = f32[16,48,128]{2,1,0:T(8,128)S(1)} all-to-all(f32[16,48,128]{2,1,0:T(8,128)S(1)} %bitcast.11), channel_id=1, replica_groups=mesh['gx'=16,'gy'=16] {'gy'}, dimensions={0} | all-to-all | bytes 786432 | tf_op jit(solution)/shard_map/all_to_all | solution.py:225
  127.2 0.0 copy-done.4
  127.2 0.0 copy-done.5
  127.2 1.4 %shard_map.113 = f32[9,4,16,256]{3,2,1,0:T(8,128)} custom-call(f32[16,3,16,128]{3,2,1,0:T(8,128)S(1)} %bitcast.10, bf16[256,768]{1,0:T(8,128)(2,1)S(1)} %copy-done.5, bf16[256,768]{1,0:T(8,128)(2,1)S(1)} %copy-done.4), custom_call_target="tpu_custom_call" | custom-call | tf_op jit(solution)/shard_map/pallas_call | solution.py:214
Async XLA Ops:
  0.0 59.2 %copy-start.2 = (bf16[2,128,1024]{2,1,0:T(8,128)(2,1)S(1)}, bf16[2,128,1024]{2,1,0:T(8,128)(2,1)}, u32[]{:S(2)}) copy-start(bf16[2,128,1024]{2,1,0:T(8,128)(2,1)} %constant.21.clone.low_ref) | copy-start | bytes 1572868
  0.0 59.2 %copy-start.3 = (bf16[2,128,1024]{2,1,0:T(8,128)(2,1)S(1)}, bf16[2,128,1024]{2,1,0:T(8,128)(2,1)}, u32[]{:S(2)}) copy-start(bf16[2,128,1024]{2,1,0:T(8,128)(2,1)} %constant.20.clone.high_ref) | copy-start | bytes 1572868
  59.2 25.1 %copy-start = (bf16[2,1024,128]{2,1,0:T(8,128)(2,1)S(1)}, bf16[2,1024,128]{2,1,0:T(8,128)(2,1)}, u32[]{:S(2)}) copy-start(bf16[2,1024,128]{2,1,0:T(8,128)(2,1)} %constant.23.clone.low_ref) | copy-start | bytes 1572868
  59.2 25.1 %copy-start.1 = (bf16[2,1024,128]{2,1,0:T(8,128)(2,1)S(1)}, bf16[2,1024,128]{2,1,0:T(8,128)(2,1)}, u32[]{:S(2)}) copy-start(bf16[2,1024,128]{2,1,0:T(8,128)(2,1)} %constant.22.clone.high_ref) | copy-start | bytes 1572868
  59.2 40.0 %copy-start.8 = (bf16[384,128]{1,0:T(8,128)(2,1)S(1)}, bf16[384,128]{1,0:T(8,128)(2,1)}, u32[]{:S(2)}) copy-start(bf16[384,128]{1,0:T(8,128)(2,1)} %constant.25.clone.low_ref) | copy-start | bytes 294916
  59.2 40.0 %copy-start.9 = (bf16[384,128]{1,0:T(8,128)(2,1)S(1)}, bf16[384,128]{1,0:T(8,128)(2,1)}, u32[]{:S(2)}) copy-start(bf16[384,128]{1,0:T(8,128)(2,1)} %constant.24.clone.high_ref) | copy-start | bytes 294916
  59.2 52.7 %copy-start.6 = (bf16[768,256]{1,0:T(8,128)(2,1)S(1)}, bf16[768,256]{1,0:T(8,128)(2,1)}, u32[]{:S(2)}) copy-start(bf16[768,256]{1,0:T(8,128)(2,1)} %constant.27.clone.low_ref) | copy-start | bytes 1179652
  59.2 52.7 %copy-start.7 = (bf16[768,256]{1,0:T(8,128)(2,1)S(1)}, bf16[768,256]{1,0:T(8,128)(2,1)}, u32[]{:S(2)}) copy-start(bf16[768,256]{1,0:T(8,128)(2,1)} %constant.26.clone.high_ref) | copy-start | bytes 1179652
  60.6 66.6 %copy-start.4 = (bf16[256,768]{1,0:T(8,128)(2,1)S(1)}, bf16[256,768]{1,0:T(8,128)(2,1)}, u32[]{:S(2)}) copy-start(bf16[256,768]{1,0:T(8,128)(2,1)} %constant.29.clone.low_ref) | copy-start | bytes 1179652
  60.6 66.6 %copy-start.5 = (bf16[256,768]{1,0:T(8,128)(2,1)S(1)}, bf16[256,768]{1,0:T(8,128)(2,1)}, u32[]{:S(2)}) copy-start(bf16[256,768]{1,0:T(8,128)(2,1)} %constant.28.clone.high_ref) | copy-start | bytes 1179652
where the time goes:
time: 129 us
  blocking collectives  124 us (96%)
  Pallas kernels  4.25 us (3%)
    all_to_all x5, blocking collectives, exchange(): return lax.all_to_all(value, axis, split_axis=0, concat_axis=0, tiled=True)  124 us
    pallas_call x5, Pallas kernels, call(): pl.pallas_call(kernel, out_shape=jax.ShapeDtypeStruct(out_shape, F32), in...  4.25 us

commit v1 on v0

--- a/solution.py
+++ b/solution.py
@@ -15,6 +15,13 @@
 MX = 256
 MY = 256
 GROUP = 16
+GX_ORDER = [2 * z + x_lo for x_lo in range(2) for z in range(8)]
+GY_ORDER = [8 * x_hi + 2 * y + core for core in range(2) for y in (0, 2, 1, 3) for x_hi in range(2)]
+LAST_ORDER = list(range(GROUP))[::-1]
+ENDS = {
+    axis: [[order.index(device + 8 * end) for device in range(8)] for end in range(2)]
+    for axis, order in (("gx", GX_ORDER), ("gy", GY_ORDER))
+}
 VMEM_LIMIT = 24 * 1024 * 1024
 F32 = jnp.float32
 BF16 = jnp.bfloat16
@@ -78,14 +85,21 @@
 
 def z_table():
     ops = np.stack([circulant_table(NZ, power) for power in range(3)])
-    ops = ops.reshape(3, GROUP, NZ // GROUP, NZ).transpose(1, 0, 2, 3).reshape(3 * NZ, NZ)
+    ops = ops.reshape(3, GROUP, NZ // GROUP, NZ).transpose(1, 0, 2, 3)[GX_ORDER].reshape(3 * NZ, NZ)
     return [np.kron(part, np.eye(2, dtype=ml_dtypes.bfloat16)) for part in split(ops, 1)]
 
 
 def y_table():
-    ops = np.concatenate([inverse_table(NY, MY, power) for power in range(3)])
+    ops = np.stack([inverse_table(NY, MY, power) for power in range(3)])
+    ops = ops.reshape(3, GROUP, -1, MY)[:, LAST_ORDER]
     ops = ops.reshape(3 * MY, GROUP, 2, 8).transpose(0, 3, 2, 1)
     return ops.reshape(3 * MY, MY)
+
+
+def x_table():
+    ops = np.concatenate([inverse_table(NX, MX, power).T for power in range(3)], axis=1)
+    blocks = [GY_ORDER.index(device) for device in LAST_ORDER]
+    return ops.reshape(GROUP, -1, 3 * MX)[blocks].reshape(MX, 3 * MX)
 
 
 def split_value(value):
@@ -123,8 +137,10 @@
 def forward_y(v_ref, high_ref, low_ref, out_ref):
     planes = v_ref.shape[1]
     ends = [
-        jnp.concatenate([v_ref[8 * e : 8 * e + 8, z].reshape(NY // 2, 128) for z in range(planes)], axis=1)
-        for e in range(2)
+        jnp.concatenate(
+            [jnp.concatenate([v_ref[k, z] for k in end], axis=0) for z in range(planes)], axis=1
+        )
+        for end in ENDS["gy"]
     ]
     for parity, lines in enumerate(fold(*ends)):
         product = dot3((high_ref[parity], low_ref[parity]), lines)
@@ -135,7 +151,7 @@
 
 def forward_x(v_ref, high_ref, low_ref, out_ref, total):
     rows = v_ref.shape[1]
-    ends = [jnp.concatenate([v_ref[8 * e + s] for s in range(8)], axis=1) for e in range(2)]
+    ends = [jnp.concatenate([v_ref[k] for k in end], axis=1) for end in ENDS["gx"]]
     for parity, (high, low) in enumerate(fold(*ends)):
         both = dot(jnp.concatenate([high, low], axis=0), high_ref[parity])
         total[parity] = both[:rows] + both[rows:] + dot(high, low_ref[parity])
@@ -221,21 +237,21 @@
     )(*operands)
 
 
-def exchange(value, axis):
-    return lax.all_to_all(value, axis, split_axis=0, concat_axis=0, tiled=True)
+def exchange(value, axis, order):
+    return lax.all_to_all(value, axis, split_axis=0, concat_axis=0, tiled=True, axis_index_groups=[order])
 
 
 def on_device(volume):
     y_high, y_low = split(folded_table(NY, MY), 2)
     x_high, x_low = split(folded_table(NX, MX).transpose(0, 2, 1), 1)
-    lines = exchange(volume.reshape(GROUP, 4 * 128, 128), "gy").reshape(GROUP, 4, 128, 128)
+    lines = exchange(volume.reshape(GROUP, 4 * 128, 128), "gy", GY_ORDER).reshape(GROUP, 4, 128, 128)
     lines = call(
         forward_y,
         (GROUP, 4, GROUP, 128),
         (lines, y_high, y_low),
     )
 
-    lines = exchange(lines.reshape(GROUP, 64, 128), "gx")
+    lines = exchange(lines.reshape(GROUP, 64, 128), "gx", GX_ORDER)
     lines = call(
         forward_x,
         (GROUP, 8, 128),
@@ -243,18 +259,17 @@
         scratch=(pltpu.VMEM((2, 64, 128), F32),),
     )
 
-    lines = exchange(lines, "gy").reshape(GROUP * 8, 128)
+    lines = exchange(lines, "gy", GY_ORDER).reshape(GROUP * 8, 128)
     lines = call(along_z, (6 * NZ, 128), (lines, *z_table()))
 
-    lines = exchange(lines.reshape(GROUP, 24, 128), "gx").reshape(6 * NZ, 128)
+    lines = exchange(lines.reshape(GROUP, 24, 128), "gx", GX_ORDER).reshape(6 * NZ, 128)
     lines = call(inverse_y, (GROUP, 3, GROUP, 128), (lines, *split(y_table())))
 
-    lines = exchange(lines.reshape(GROUP, 48, 128), "gy").reshape(GROUP, 3, GROUP, 128)
-    back_x = np.concatenate([inverse_table(NX, MX, power).T for power in range(3)], axis=1)
+    lines = exchange(lines.reshape(GROUP, 48, 128), "gy", LAST_ORDER).reshape(GROUP, 3, GROUP, 128)
     return call(
         inverse_x,
         (9, 4, GROUP, MX),
-        (lines, *split(back_x)),
+        (lines, *split(x_table())),
         out_specs=pl.BlockSpec(memory_space=pl.ANY),
         scratch=(pltpu.VMEM((9, 4, GROUP, MX), F32), pltpu.SemaphoreType.DMA((9,))),
     )

time: 129 us -> 125 us (0.969)
  blocking collectives: 124 us -> 120 us
    all_to_all x5, blocking collectives: 124 us -> 120 us  [exchange(): lax.all_to_all(value, axis, split_axis=0, concat_axis=0, tiled=True, axis...]
where the time goes in v1:
time: 125 us
  blocking collectives  120 us (96%)
  Pallas kernels  4.24 us (3%)
    all_to_all x5, blocking collectives, exchange(): lax.all_to_all(value, axis, split_axis=0, concat_axis=0, tiled=True, axis...  120 us
    pallas_call x5, Pallas kernels, call(): pl.pallas_call(kernel, out_shape=jax.ShapeDtypeStruct(out_shape, F32), in...  4.24 us

profile of v1, /device:TPU:1, one launch (start us, length us, event | category | flops | bytes accessed | tf_op | source)
XLA Modules:
  0.0 124.8 jit_solution(7001452014630674155)
XLA Ops:
  0.0 0.0 copy-start.2
  0.0 0.0 copy-start.3
  0.0 58.8 %all_to_all.25 = f32[16,512,128]{2,1,0:T(8,128)S(1)} all-to-all(f32[16,512,128]{2,1,0:T(8,128)} %bitcast.15), channel_id=1, replica_groups={{0,8,4,12,2,10,6,14,1,9,5,13,3,11,7,15},{16,24,20,28,18,26,22,30,17,25,..., dimensions={0} | all-to-all | bytes 8388608 | tf_op jit(solution)/shard_map/all_to_all | solution.py:241
  58.8 0.0 copy-start
  58.8 0.0 copy-start.1
  58.8 0.0 copy-done.2
  58.8 0.0 copy-done.3
  58.8 0.0 copy-start.8
  58.8 0.0 copy-start.9
  58.8 0.0 copy-start.6
  58.8 0.0 copy-start.7
  58.8 1.3 %shard_map.109 = f32[16,4,16,128]{3,2,1,0:T(8,128)S(1)} custom-call(f32[16,4,128,128]{3,2,1,0:T(8,128)S(1)} %bitcast.8, bf16[2,128,1024]{2,1,0:T(8,128)(2,1)S(1)} %copy-done.3, bf16[2,128,1024]{2,1,0:T(8,128)(2,1)S(1)} %copy-done.2), custom_call_target="tpu_custom_call" | custom-call | tf_op jit(solution)/shard_map/pallas_call | solution.py:230
  60.2 0.0 copy-start.4
  60.2 0.0 copy-start.5
  60.2 21.5 %all_to_all.26.v_ref = f32[16,64,128]{2,1,0:T(8,128)S(1)} all-to-all(f32[16,64,128]{2,1,0:T(8,128)S(1)} %bitcast.9), channel_id=1, replica_groups={{0,32,64,96,128,160,192,224,16,48,80,112,144,176,208,240},{1,33,65,97,1..., dimensions={0} | all-to-all | bytes 1048576 | tf_op jit(solution)/shard_map/all_to_all | solution.py:241
  81.6 0.0 copy-done
  81.6 0.0 copy-done.1
  81.6 0.6 shard_map.110
  82.2 13.5 %all_to_all.27 = f32[16,8,128]{2,1,0:T(8,128)S(1)} all-to-all(f32[16,8,128]{2,1,0:T(8,128)S(1)} %shard_map.110), channel_id=1, replica_groups={{0,8,4,12,2,10,6,14,1,9,5,13,3,11,7,15},{16,24,20,28,18,26,22,30,17,25,..., dimensions={0} | all-to-all | bytes 131072 | tf_op jit(solution)/shard_map/all_to_all | solution.py:241
  95.7 0.0 copy-done.8
  95.7 0.0 copy-done.9
  95.7 0.2 shard_map.111
  95.9 11.6 %all_to_all.28 = f32[16,24,128]{2,1,0:T(8,128)S(1)} all-to-all(f32[16,24,128]{2,1,0:T(8,128)S(1)} %bitcast.12), channel_id=1, replica_groups={{0,32,64,96,128,160,192,224,16,48,80,112,144,176,208,240},{1,33,65,97,1..., dimensions={0} | all-to-all | bytes 393216 | tf_op jit(solution)/shard_map/all_to_all | solution.py:241
  107.6 0.0 copy-done.6
  107.6 0.0 copy-done.7
  107.6 0.7 shard_map.112
  108.3 15.1 %all_to_all.29 = f32[16,48,128]{2,1,0:T(8,128)S(1)} all-to-all(f32[16,48,128]{2,1,0:T(8,128)S(1)} %bitcast.11), channel_id=1, replica_groups={{15,14,13,12,11,10,9,8,7,6,5,4,3,2,1,0},{31,30,29,28,27,26,25,24,23,22,..., dimensions={0} | all-to-all | bytes 786432 | tf_op jit(solution)/shard_map/all_to_all | solution.py:241
  123.4 0.0 copy-done.4
  123.4 0.0 copy-done.5
  123.4 1.4 %shard_map.113 = f32[9,4,16,256]{3,2,1,0:T(8,128)} custom-call(f32[16,3,16,128]{3,2,1,0:T(8,128)S(1)} %bitcast.10, bf16[256,768]{1,0:T(8,128)(2,1)S(1)} %copy-done.5, bf16[256,768]{1,0:T(8,128)(2,1)S(1)} %copy-done.4), custom_call_target="tpu_custom_call" | custom-call | tf_op jit(solution)/shard_map/pallas_call | solution.py:230
Async XLA Ops:
  0.0 58.8 %copy-start.2 = (bf16[2,128,1024]{2,1,0:T(8,128)(2,1)S(1)}, bf16[2,128,1024]{2,1,0:T(8,128)(2,1)}, u32[]{:S(2)}) copy-start(bf16[2,128,1024]{2,1,0:T(8,128)(2,1)} %constant.21.clone.low_ref) | copy-start | bytes 1572868
  0.0 58.8 %copy-start.3 = (bf16[2,128,1024]{2,1,0:T(8,128)(2,1)S(1)}, bf16[2,128,1024]{2,1,0:T(8,128)(2,1)}, u32[]{:S(2)}) copy-start(bf16[2,128,1024]{2,1,0:T(8,128)(2,1)} %constant.20.clone.high_ref) | copy-start | bytes 1572868
  58.8 22.9 %copy-start = (bf16[2,1024,128]{2,1,0:T(8,128)(2,1)S(1)}, bf16[2,1024,128]{2,1,0:T(8,128)(2,1)}, u32[]{:S(2)}) copy-start(bf16[2,1024,128]{2,1,0:T(8,128)(2,1)} %constant.23.clone.low_ref) | copy-start | bytes 1572868
  58.8 22.9 %copy-start.1 = (bf16[2,1024,128]{2,1,0:T(8,128)(2,1)S(1)}, bf16[2,1024,128]{2,1,0:T(8,128)(2,1)}, u32[]{:S(2)}) copy-start(bf16[2,1024,128]{2,1,0:T(8,128)(2,1)} %constant.22.clone.high_ref) | copy-start | bytes 1572868
  58.8 36.9 %copy-start.8 = (bf16[384,128]{1,0:T(8,128)(2,1)S(1)}, bf16[384,128]{1,0:T(8,128)(2,1)}, u32[]{:S(2)}) copy-start(bf16[384,128]{1,0:T(8,128)(2,1)} %constant.25.clone.low_ref) | copy-start | bytes 294916
  58.8 36.9 %copy-start.9 = (bf16[384,128]{1,0:T(8,128)(2,1)S(1)}, bf16[384,128]{1,0:T(8,128)(2,1)}, u32[]{:S(2)}) copy-start(bf16[384,128]{1,0:T(8,128)(2,1)} %constant.24.clone.high_ref) | copy-start | bytes 294916
  58.8 48.7 %copy-start.6 = (bf16[768,256]{1,0:T(8,128)(2,1)S(1)}, bf16[768,256]{1,0:T(8,128)(2,1)}, u32[]{:S(2)}) copy-start(bf16[768,256]{1,0:T(8,128)(2,1)} %constant.27.clone.low_ref) | copy-start | bytes 1179652
  58.8 48.7 %copy-start.7 = (bf16[768,256]{1,0:T(8,128)(2,1)S(1)}, bf16[768,256]{1,0:T(8,128)(2,1)}, u32[]{:S(2)}) copy-start(bf16[768,256]{1,0:T(8,128)(2,1)} %constant.26.clone.high_ref) | copy-start | bytes 1179652
  60.2 63.2 %copy-start.4 = (bf16[256,768]{1,0:T(8,128)(2,1)S(1)}, bf16[256,768]{1,0:T(8,128)(2,1)}, u32[]{:S(2)}) copy-start(bf16[256,768]{1,0:T(8,128)(2,1)} %constant.29.clone.low_ref) | copy-start | bytes 1179652
  60.2 63.2 %copy-start.5 = (bf16[256,768]{1,0:T(8,128)(2,1)S(1)}, bf16[256,768]{1,0:T(8,128)(2,1)}, u32[]{:S(2)}) copy-start(bf16[256,768]{1,0:T(8,128)(2,1)} %constant.28.clone.high_ref) | copy-start | bytes 1179652

commit v2 on v1

--- a/solution.py
+++ b/solution.py
@@ -17,7 +17,7 @@
 GROUP = 16
 GX_ORDER = [2 * z + x_lo for x_lo in range(2) for z in range(8)]
 GY_ORDER = [8 * x_hi + 2 * y + core for core in range(2) for y in (0, 2, 1, 3) for x_hi in range(2)]
-LAST_ORDER = list(range(GROUP))[::-1]
+LAST_ORDER = [3, 14, 7, 9, 13, 11, 4, 5, 12, 8, 1, 0, 15, 6, 2, 10]
 ENDS = {
     axis: [[order.index(device + 8 * end) for device in range(8)] for end in range(2)]
     for axis, order in (("gx", GX_ORDER), ("gy", GY_ORDER))

time: 125 us -> 125 us (level)
  no operation moved by 1% of the time
where the time goes in v2:
time: 125 us
  blocking collectives  121 us (97%)
  Pallas kernels  4.24 us (3%)
    all_to_all x5, blocking collectives, exchange(): lax.all_to_all(value, axis, split_axis=0, concat_axis=0, tiled=True, axis...  121 us
    pallas_call x5, Pallas kernels, call(): pl.pallas_call(kernel, out_shape=jax.ShapeDtypeStruct(out_shape, F32), in...  4.24 us

profile of v2, /device:TPU:1, one launch (start us, length us, event | category | flops | bytes accessed | tf_op | source)
XLA Modules:
  0.0 125.1 jit_solution(12037503425360827410)
XLA Ops:
  0.0 0.0 copy-start.2
  0.0 0.0 copy-start.3
  0.0 58.8 %all_to_all.25 = f32[16,512,128]{2,1,0:T(8,128)S(1)} all-to-all(f32[16,512,128]{2,1,0:T(8,128)} %bitcast.15), channel_id=1, replica_groups={{0,8,4,12,2,10,6,14,1,9,5,13,3,11,7,15},{16,24,20,28,18,26,22,30,17,25,..., dimensions={0} | all-to-all | bytes 8388608 | tf_op jit(solution)/shard_map/all_to_all | solution.py:241
  58.8 0.0 copy-start
  58.8 0.0 copy-start.1
  58.8 0.0 copy-done.2
  58.8 0.0 copy-done.3
  58.8 0.0 copy-start.8
  58.8 0.0 copy-start.9
  58.8 0.0 copy-start.6
  58.8 0.0 copy-start.7
  58.8 1.3 %shard_map.109 = f32[16,4,16,128]{3,2,1,0:T(8,128)S(1)} custom-call(f32[16,4,128,128]{3,2,1,0:T(8,128)S(1)} %bitcast.8, bf16[2,128,1024]{2,1,0:T(8,128)(2,1)S(1)} %copy-done.3, bf16[2,128,1024]{2,1,0:T(8,128)(2,1)S(1)} %copy-done.2), custom_call_target="tpu_custom_call" | custom-call | tf_op jit(solution)/shard_map/pallas_call | solution.py:230
  60.2 0.0 copy-start.4
  60.2 0.0 copy-start.5
  60.2 21.5 %all_to_all.26.v_ref = f32[16,64,128]{2,1,0:T(8,128)S(1)} all-to-all(f32[16,64,128]{2,1,0:T(8,128)S(1)} %bitcast.9), channel_id=1, replica_groups={{0,32,64,96,128,160,192,224,16,48,80,112,144,176,208,240},{1,33,65,97,1..., dimensions={0} | all-to-all | bytes 1048576 | tf_op jit(solution)/shard_map/all_to_all | solution.py:241
  81.6 0.0 copy-done
  81.6 0.0 copy-done.1
  81.6 0.6 shard_map.110
  82.2 13.5 %all_to_all.27 = f32[16,8,128]{2,1,0:T(8,128)S(1)} all-to-all(f32[16,8,128]{2,1,0:T(8,128)S(1)} %shard_map.110), channel_id=1, replica_groups={{0,8,4,12,2,10,6,14,1,9,5,13,3,11,7,15},{16,24,20,28,18,26,22,30,17,25,..., dimensions={0} | all-to-all | bytes 131072 | tf_op jit(solution)/shard_map/all_to_all | solution.py:241
  95.7 0.0 copy-done.8
  95.7 0.0 copy-done.9
  95.7 0.2 shard_map.111
  95.9 11.6 %all_to_all.28 = f32[16,24,128]{2,1,0:T(8,128)S(1)} all-to-all(f32[16,24,128]{2,1,0:T(8,128)S(1)} %bitcast.12), channel_id=1, replica_groups={{0,32,64,96,128,160,192,224,16,48,80,112,144,176,208,240},{1,33,65,97,1..., dimensions={0} | all-to-all | bytes 393216 | tf_op jit(solution)/shard_map/all_to_all | solution.py:241
  107.6 0.0 copy-done.6
  107.6 0.0 copy-done.7
  107.6 0.7 shard_map.112
  108.3 15.4 %all_to_all.29 = f32[16,48,128]{2,1,0:T(8,128)S(1)} all-to-all(f32[16,48,128]{2,1,0:T(8,128)S(1)} %bitcast.11), channel_id=1, replica_groups={{3,14,7,9,13,11,4,5,12,8,1,0,15,6,2,10},{19,30,23,25,29,27,20,21,28,24,..., dimensions={0} | all-to-all | bytes 786432 | tf_op jit(solution)/shard_map/all_to_all | solution.py:241
  123.7 0.0 copy-done.4
  123.7 0.0 copy-done.5
  123.7 1.4 %shard_map.113 = f32[9,4,16,256]{3,2,1,0:T(8,128)} custom-call(f32[16,3,16,128]{3,2,1,0:T(8,128)S(1)} %bitcast.10, bf16[256,768]{1,0:T(8,128)(2,1)S(1)} %copy-done.5, bf16[256,768]{1,0:T(8,128)(2,1)S(1)} %copy-done.4), custom_call_target="tpu_custom_call" | custom-call | tf_op jit(solution)/shard_map/pallas_call | solution.py:230
Async XLA Ops:
  0.0 58.8 %copy-start.2 = (bf16[2,128,1024]{2,1,0:T(8,128)(2,1)S(1)}, bf16[2,128,1024]{2,1,0:T(8,128)(2,1)}, u32[]{:S(2)}) copy-start(bf16[2,128,1024]{2,1,0:T(8,128)(2,1)} %constant.21.clone.low_ref) | copy-start | bytes 1572868
  0.0 58.8 %copy-start.3 = (bf16[2,128,1024]{2,1,0:T(8,128)(2,1)S(1)}, bf16[2,128,1024]{2,1,0:T(8,128)(2,1)}, u32[]{:S(2)}) copy-start(bf16[2,128,1024]{2,1,0:T(8,128)(2,1)} %constant.20.clone.high_ref) | copy-start | bytes 1572868
  58.8 22.9 %copy-start = (bf16[2,1024,128]{2,1,0:T(8,128)(2,1)S(1)}, bf16[2,1024,128]{2,1,0:T(8,128)(2,1)}, u32[]{:S(2)}) copy-start(bf16[2,1024,128]{2,1,0:T(8,128)(2,1)} %constant.23.clone.low_ref) | copy-start | bytes 1572868
  58.8 22.9 %copy-start.1 = (bf16[2,1024,128]{2,1,0:T(8,128)(2,1)S(1)}, bf16[2,1024,128]{2,1,0:T(8,128)(2,1)}, u32[]{:S(2)}) copy-start(bf16[2,1024,128]{2,1,0:T(8,128)(2,1)} %constant.22.clone.high_ref) | copy-start | bytes 1572868
  58.8 36.9 %copy-start.8 = (bf16[384,128]{1,0:T(8,128)(2,1)S(1)}, bf16[384,128]{1,0:T(8,128)(2,1)}, u32[]{:S(2)}) copy-start(bf16[384,128]{1,0:T(8,128)(2,1)} %constant.25.clone.low_ref) | copy-start | bytes 294916
  58.8 36.9 %copy-start.9 = (bf16[384,128]{1,0:T(8,128)(2,1)S(1)}, bf16[384,128]{1,0:T(8,128)(2,1)}, u32[]{:S(2)}) copy-start(bf16[384,128]{1,0:T(8,128)(2,1)} %constant.24.clone.high_ref) | copy-start | bytes 294916
  58.8 48.7 %copy-start.6 = (bf16[768,256]{1,0:T(8,128)(2,1)S(1)}, bf16[768,256]{1,0:T(8,128)(2,1)}, u32[]{:S(2)}) copy-start(bf16[768,256]{1,0:T(8,128)(2,1)} %constant.27.clone.low_ref) | copy-start | bytes 1179652
  58.8 48.7 %copy-start.7 = (bf16[768,256]{1,0:T(8,128)(2,1)S(1)}, bf16[768,256]{1,0:T(8,128)(2,1)}, u32[]{:S(2)}) copy-start(bf16[768,256]{1,0:T(8,128)(2,1)} %constant.26.clone.high_ref) | copy-start | bytes 1179652
  60.2 63.6 %copy-start.4 = (bf16[256,768]{1,0:T(8,128)(2,1)S(1)}, bf16[256,768]{1,0:T(8,128)(2,1)}, u32[]{:S(2)}) copy-start(bf16[256,768]{1,0:T(8,128)(2,1)} %constant.29.clone.low_ref) | copy-start | bytes 1179652
  60.2 63.5 %copy-start.5 = (bf16[256,768]{1,0:T(8,128)(2,1)S(1)}, bf16[256,768]{1,0:T(8,128)(2,1)}, u32[]{:S(2)}) copy-start(bf16[256,768]{1,0:T(8,128)(2,1)} %constant.28.clone.high_ref) | copy-start | bytes 1179652

commit v3 on v2

--- a/solution.py
+++ b/solution.py
@@ -16,7 +16,7 @@
 MY = 256
 GROUP = 16
 GX_ORDER = [2 * z + x_lo for x_lo in range(2) for z in range(8)]
-GY_ORDER = [8 * x_hi + 2 * y + core for core in range(2) for y in (0, 2, 1, 3) for x_hi in range(2)]
+GY_ORDER = [8 * x_hi + 2 * y + core for core in (1, 0) for y in (0, 2, 1, 3) for x_hi in range(2)]
 LAST_ORDER = [3, 14, 7, 9, 13, 11, 4, 5, 12, 8, 1, 0, 15, 6, 2, 10]
 ENDS = {
     axis: [[order.index(device + 8 * end) for device in range(8)] for end in range(2)]

time: 125 us -> 125 us (level)
  no operation moved by 1% of the time
where the time goes in v3:
time: 125 us
  blocking collectives  120 us (96%)
  Pallas kernels  4.25 us (3%)
    all_to_all x5, blocking collectives, exchange(): lax.all_to_all(value, axis, split_axis=0, concat_axis=0, tiled=True, axis...  120 us
    pallas_call x5, Pallas kernels, call(): pl.pallas_call(kernel, out_shape=jax.ShapeDtypeStruct(out_shape, F32), in...  4.25 us

profile of v3, /device:TPU:1, one launch (start us, length us, event | category | flops | bytes accessed | tf_op | source)
XLA Modules:
  0.0 124.6 jit_solution(3299918426185512619)
XLA Ops:
  0.0 0.0 copy-start.2
  0.0 0.0 copy-start.3
  0.0 58.4 %all_to_all.25 = f32[16,512,128]{2,1,0:T(8,128)S(1)} all-to-all(f32[16,512,128]{2,1,0:T(8,128)} %bitcast.15), channel_id=1, replica_groups={{1,9,5,13,3,11,7,15,0,8,4,12,2,10,6,14},{17,25,21,29,19,27,23,31,16,24,..., dimensions={0} | all-to-all | bytes 8388608 | tf_op jit(solution)/shard_map/all_to_all | solution.py:241
  58.4 0.0 copy-start
  58.4 0.0 copy-start.1
  58.4 0.0 copy-done.2
  58.4 0.0 copy-done.3
  58.4 0.0 copy-start.8
  58.4 0.0 copy-start.9
  58.4 0.0 copy-start.6
  58.4 0.0 copy-start.7
  58.5 1.3 %shard_map.109 = f32[16,4,16,128]{3,2,1,0:T(8,128)S(1)} custom-call(f32[16,4,128,128]{3,2,1,0:T(8,128)S(1)} %bitcast.8, bf16[2,128,1024]{2,1,0:T(8,128)(2,1)S(1)} %copy-done.3, bf16[2,128,1024]{2,1,0:T(8,128)(2,1)S(1)} %copy-done.2), custom_call_target="tpu_custom_call" | custom-call | tf_op jit(solution)/shard_map/pallas_call | solution.py:230
  59.8 0.0 copy-start.4
  59.8 0.0 copy-start.5
  59.8 21.5 %all_to_all.26.v_ref = f32[16,64,128]{2,1,0:T(8,128)S(1)} all-to-all(f32[16,64,128]{2,1,0:T(8,128)S(1)} %bitcast.9), channel_id=1, replica_groups={{0,32,64,96,128,160,192,224,16,48,80,112,144,176,208,240},{1,33,65,97,1..., dimensions={0} | all-to-all | bytes 1048576 | tf_op jit(solution)/shard_map/all_to_all | solution.py:241
  81.3 0.0 copy-done
  81.3 0.0 copy-done.1
  81.3 0.6 shard_map.110
  81.9 13.5 %all_to_all.27 = f32[16,8,128]{2,1,0:T(8,128)S(1)} all-to-all(f32[16,8,128]{2,1,0:T(8,128)S(1)} %shard_map.110), channel_id=1, replica_groups={{1,9,5,13,3,11,7,15,0,8,4,12,2,10,6,14},{17,25,21,29,19,27,23,31,16,24,..., dimensions={0} | all-to-all | bytes 131072 | tf_op jit(solution)/shard_map/all_to_all | solution.py:241
  95.4 0.0 copy-done.8
  95.4 0.0 copy-done.9
  95.4 0.2 shard_map.111
  95.6 11.6 %all_to_all.28 = f32[16,24,128]{2,1,0:T(8,128)S(1)} all-to-all(f32[16,24,128]{2,1,0:T(8,128)S(1)} %bitcast.12), channel_id=1, replica_groups={{0,32,64,96,128,160,192,224,16,48,80,112,144,176,208,240},{1,33,65,97,1..., dimensions={0} | all-to-all | bytes 393216 | tf_op jit(solution)/shard_map/all_to_all | solution.py:241
  107.2 0.0 copy-done.6
  107.2 0.0 copy-done.7
  107.2 0.7 shard_map.112
  107.9 15.3 %all_to_all.29 = f32[16,48,128]{2,1,0:T(8,128)S(1)} all-to-all(f32[16,48,128]{2,1,0:T(8,128)S(1)} %bitcast.11), channel_id=1, replica_groups={{3,14,7,9,13,11,4,5,12,8,1,0,15,6,2,10},{19,30,23,25,29,27,20,21,28,24,..., dimensions={0} | all-to-all | bytes 786432 | tf_op jit(solution)/shard_map/all_to_all | solution.py:241
  123.2 0.0 copy-done.4
  123.2 0.0 copy-done.5
  123.2 1.4 %shard_map.113 = f32[9,4,16,256]{3,2,1,0:T(8,128)} custom-call(f32[16,3,16,128]{3,2,1,0:T(8,128)S(1)} %bitcast.10, bf16[256,768]{1,0:T(8,128)(2,1)S(1)} %copy-done.5, bf16[256,768]{1,0:T(8,128)(2,1)S(1)} %copy-done.4), custom_call_target="tpu_custom_call" | custom-call | tf_op jit(solution)/shard_map/pallas_call | solution.py:230
Async XLA Ops:
  0.0 58.4 %copy-start.2 = (bf16[2,128,1024]{2,1,0:T(8,128)(2,1)S(1)}, bf16[2,128,1024]{2,1,0:T(8,128)(2,1)}, u32[]{:S(2)}) copy-start(bf16[2,128,1024]{2,1,0:T(8,128)(2,1)} %constant.21.clone.low_ref) | copy-start | bytes 1572868
  0.0 58.4 %copy-start.3 = (bf16[2,128,1024]{2,1,0:T(8,128)(2,1)S(1)}, bf16[2,128,1024]{2,1,0:T(8,128)(2,1)}, u32[]{:S(2)}) copy-start(bf16[2,128,1024]{2,1,0:T(8,128)(2,1)} %constant.20.clone.high_ref) | copy-start | bytes 1572868
  58.4 22.9 %copy-start = (bf16[2,1024,128]{2,1,0:T(8,128)(2,1)S(1)}, bf16[2,1024,128]{2,1,0:T(8,128)(2,1)}, u32[]{:S(2)}) copy-start(bf16[2,1024,128]{2,1,0:T(8,128)(2,1)} %constant.23.clone.low_ref) | copy-start | bytes 1572868
  58.4 22.9 %copy-start.1 = (bf16[2,1024,128]{2,1,0:T(8,128)(2,1)S(1)}, bf16[2,1024,128]{2,1,0:T(8,128)(2,1)}, u32[]{:S(2)}) copy-start(bf16[2,1024,128]{2,1,0:T(8,128)(2,1)} %constant.22.clone.high_ref) | copy-start | bytes 1572868
  58.4 37.0 %copy-start.8 = (bf16[384,128]{1,0:T(8,128)(2,1)S(1)}, bf16[384,128]{1,0:T(8,128)(2,1)}, u32[]{:S(2)}) copy-start(bf16[384,128]{1,0:T(8,128)(2,1)} %constant.25.clone.low_ref) | copy-start | bytes 294916
  58.4 37.0 %copy-start.9 = (bf16[384,128]{1,0:T(8,128)(2,1)S(1)}, bf16[384,128]{1,0:T(8,128)(2,1)}, u32[]{:S(2)}) copy-start(bf16[384,128]{1,0:T(8,128)(2,1)} %constant.24.clone.high_ref) | copy-start | bytes 294916
  58.4 48.8 %copy-start.6 = (bf16[768,256]{1,0:T(8,128)(2,1)S(1)}, bf16[768,256]{1,0:T(8,128)(2,1)}, u32[]{:S(2)}) copy-start(bf16[768,256]{1,0:T(8,128)(2,1)} %constant.27.clone.low_ref) | copy-start | bytes 1179652
  58.4 48.7 %copy-start.7 = (bf16[768,256]{1,0:T(8,128)(2,1)S(1)}, bf16[768,256]{1,0:T(8,128)(2,1)}, u32[]{:S(2)}) copy-start(bf16[768,256]{1,0:T(8,128)(2,1)} %constant.26.clone.high_ref) | copy-start | bytes 1179652
  59.8 63.4 %copy-start.4 = (bf16[256,768]{1,0:T(8,128)(2,1)S(1)}, bf16[256,768]{1,0:T(8,128)(2,1)}, u32[]{:S(2)}) copy-start(bf16[256,768]{1,0:T(8,128)(2,1)} %constant.29.clone.low_ref) | copy-start | bytes 1179652
  59.8 63.4 %copy-start.5 = (bf16[256,768]{1,0:T(8,128)(2,1)S(1)}, bf16[256,768]{1,0:T(8,128)(2,1)}, u32[]{:S(2)}) copy-start(bf16[256,768]{1,0:T(8,128)(2,1)} %constant.28.clone.high_ref) | copy-start | bytes 1179652

commit v4 on v3

--- a/solution.py
+++ b/solution.py
@@ -115,6 +115,12 @@
     return dot(a[0], b[0]) + dot(a[0], b[1]) + dot(a[1], b[0])
 
 
+def stacked_dot3(a, b):
+    rows = a[0].shape[0]
+    both = dot(jnp.concatenate(a, axis=0), b[0])
+    return both[:rows] + both[rows:] + dot(a[0], b[1])
+
+
 def swap_blocks(arrays):
     block = lax.broadcasted_iota(jnp.int32, arrays[0].shape, 1) // 16
     arrays = list(arrays)
@@ -143,20 +149,18 @@
         for end in ENDS["gy"]
     ]
     for parity, lines in enumerate(fold(*ends)):
-        product = dot3((high_ref[parity], low_ref[parity]), lines)
+        product = stacked_dot3((high_ref[parity], low_ref[parity]), lines)
         for z in range(planes):
             piece = product[:, 128 * z : 128 * (z + 1)].reshape(GROUP // 2, GROUP, 128)
             out_ref[8 * parity : 8 * parity + 8, z] = piece
 
 
 def forward_x(v_ref, high_ref, low_ref, out_ref, total):
-    rows = v_ref.shape[1]
     ends = [jnp.concatenate([v_ref[k] for k in end], axis=1) for end in ENDS["gx"]]
-    for parity, (high, low) in enumerate(fold(*ends)):
-        both = dot(jnp.concatenate([high, low], axis=0), high_ref[parity])
-        total[parity] = both[:rows] + both[rows:] + dot(high, low_ref[parity])
-        lines = [total[parity, pl.ds(q, 8, stride=8), :] for q in range(8)]
-        for k, message in enumerate(swap_blocks(lines)):
+    for parity, lines in enumerate(fold(*ends)):
+        total[parity] = stacked_dot3(lines, (high_ref[parity], low_ref[parity]))
+        groups = [total[parity, pl.ds(q, 8, stride=8), :] for q in range(8)]
+        for k, message in enumerate(swap_blocks(groups)):
             out_ref[8 * parity + k] = message
 
 
@@ -212,7 +216,7 @@
             low_ref[:, MX * power : MX * (power + 1)],
         )
         lines = jnp.concatenate([combos[PLACES[yz]] for _, yz in FIELDS[power]], axis=0)
-        product = dot3(split_value(lines), table)
+        product = stacked_dot3(split_value(lines), table)
         for n, (field, _) in enumerate(FIELDS[power]):
             for z in range(4):
                 start = 64 * n + 16 * z

time: 125 us -> 125 us (level)
  no operation moved by 1% of the time
where the time goes in v4:
time: 125 us; the launch traced here: 124 us
  blocking collectives  120 us (96%)
  Pallas kernels  4.14 us (3%)
    all_to_all x5, blocking collectives, exchange(): lax.all_to_all(value, axis, split_axis=0, concat_axis=0, tiled=True, axis...  120 us
    pallas_call x5, Pallas kernels, call(): pl.pallas_call(kernel, out_shape=jax.ShapeDtypeStruct(out_shape, F32), in...  4.14 us

profile of v4, /device:TPU:1, one launch (start us, length us, event | category | flops | bytes accessed | tf_op | source)
XLA Modules:
  0.0 124.5 jit_solution(12070865543386606137)
XLA Ops:
  0.0 0.0 copy-start.2
  0.0 0.0 copy-start.3
  0.0 58.4 %all_to_all.25 = f32[16,512,128]{2,1,0:T(8,128)S(1)} all-to-all(f32[16,512,128]{2,1,0:T(8,128)} %bitcast.15), channel_id=1, replica_groups={{1,9,5,13,3,11,7,15,0,8,4,12,2,10,6,14},{17,25,21,29,19,27,23,31,16,24,..., dimensions={0} | all-to-all | bytes 8388608 | tf_op jit(solution)/shard_map/all_to_all | solution.py:245
  58.4 0.0 copy-start
  58.4 0.0 copy-start.1
  58.4 0.0 copy-done.2
  58.4 0.0 copy-done.3
  58.4 0.0 copy-start.8
  58.4 0.0 copy-start.9
  58.4 0.0 copy-start.6
  58.4 0.0 copy-start.7
  58.5 1.2 shard_map.109
  59.7 0.0 copy-start.4
  59.7 0.0 copy-start.5
  59.7 21.5 %all_to_all.26.v_ref = f32[16,64,128]{2,1,0:T(8,128)S(1)} all-to-all(f32[16,64,128]{2,1,0:T(8,128)S(1)} %bitcast.9), channel_id=1, replica_groups={{0,32,64,96,128,160,192,224,16,48,80,112,144,176,208,240},{1,33,65,97,1..., dimensions={0} | all-to-all | bytes 1048576 | tf_op jit(solution)/shard_map/all_to_all | solution.py:245
  81.2 0.0 copy-done
  81.2 0.0 copy-done.1
  81.2 0.6 shard_map.110
  81.7 13.5 %all_to_all.27 = f32[16,8,128]{2,1,0:T(8,128)S(1)} all-to-all(f32[16,8,128]{2,1,0:T(8,128)S(1)} %shard_map.110), channel_id=1, replica_groups={{1,9,5,13,3,11,7,15,0,8,4,12,2,10,6,14},{17,25,21,29,19,27,23,31,16,24,..., dimensions={0} | all-to-all | bytes 131072 | tf_op jit(solution)/shard_map/all_to_all | solution.py:245
  95.2 0.0 copy-done.8
  95.2 0.0 copy-done.9
  95.2 0.2 shard_map.111
  95.5 11.6 %all_to_all.28 = f32[16,24,128]{2,1,0:T(8,128)S(1)} all-to-all(f32[16,24,128]{2,1,0:T(8,128)S(1)} %bitcast.12), channel_id=1, replica_groups={{0,32,64,96,128,160,192,224,16,48,80,112,144,176,208,240},{1,33,65,97,1..., dimensions={0} | all-to-all | bytes 393216 | tf_op jit(solution)/shard_map/all_to_all | solution.py:245
  107.1 0.0 copy-done.6
  107.1 0.0 copy-done.7
  107.1 0.7 shard_map.112
  107.8 15.3 %all_to_all.29 = f32[16,48,128]{2,1,0:T(8,128)S(1)} all-to-all(f32[16,48,128]{2,1,0:T(8,128)S(1)} %bitcast.11), channel_id=1, replica_groups={{3,14,7,9,13,11,4,5,12,8,1,0,15,6,2,10},{19,30,23,25,29,27,20,21,28,24,..., dimensions={0} | all-to-all | bytes 786432 | tf_op jit(solution)/shard_map/all_to_all | solution.py:245
  123.0 0.0 copy-done.4
  123.0 0.0 copy-done.5
  123.0 1.4 %shard_map.113 = f32[9,4,16,256]{3,2,1,0:T(8,128)} custom-call(f32[16,3,16,128]{3,2,1,0:T(8,128)S(1)} %bitcast.10, bf16[256,768]{1,0:T(8,128)(2,1)S(1)} %copy-done.5, bf16[256,768]{1,0:T(8,128)(2,1)S(1)} %copy-done.4), custom_call_target="tpu_custom_call" | custom-call | tf_op jit(solution)/shard_map/pallas_call | solution.py:234
Async XLA Ops:
  0.0 58.4 %copy-start.2 = (bf16[2,128,1024]{2,1,0:T(8,128)(2,1)S(1)}, bf16[2,128,1024]{2,1,0:T(8,128)(2,1)}, u32[]{:S(2)}) copy-start(bf16[2,128,1024]{2,1,0:T(8,128)(2,1)} %constant.21.clone.low_ref) | copy-start | bytes 1572868
  0.0 58.4 %copy-start.3 = (bf16[2,128,1024]{2,1,0:T(8,128)(2,1)S(1)}, bf16[2,128,1024]{2,1,0:T(8,128)(2,1)}, u32[]{:S(2)}) copy-start(bf16[2,128,1024]{2,1,0:T(8,128)(2,1)} %constant.20.clone.high_ref) | copy-start | bytes 1572868
  58.4 22.8 %copy-start = (bf16[2,1024,128]{2,1,0:T(8,128)(2,1)S(1)}, bf16[2,1024,128]{2,1,0:T(8,128)(2,1)}, u32[]{:S(2)}) copy-start(bf16[2,1024,128]{2,1,0:T(8,128)(2,1)} %constant.23.clone.low_ref) | copy-start | bytes 1572868
  58.4 22.8 %copy-start.1 = (bf16[2,1024,128]{2,1,0:T(8,128)(2,1)S(1)}, bf16[2,1024,128]{2,1,0:T(8,128)(2,1)}, u32[]{:S(2)}) copy-start(bf16[2,1024,128]{2,1,0:T(8,128)(2,1)} %constant.22.clone.high_ref) | copy-start | bytes 1572868
  58.4 36.8 %copy-start.8 = (bf16[384,128]{1,0:T(8,128)(2,1)S(1)}, bf16[384,128]{1,0:T(8,128)(2,1)}, u32[]{:S(2)}) copy-start(bf16[384,128]{1,0:T(8,128)(2,1)} %constant.25.clone.low_ref) | copy-start | bytes 294916
  58.4 36.8 %copy-start.9 = (bf16[384,128]{1,0:T(8,128)(2,1)S(1)}, bf16[384,128]{1,0:T(8,128)(2,1)}, u32[]{:S(2)}) copy-start(bf16[384,128]{1,0:T(8,128)(2,1)} %constant.24.clone.high_ref) | copy-start | bytes 294916
  58.4 48.6 %copy-start.6 = (bf16[768,256]{1,0:T(8,128)(2,1)S(1)}, bf16[768,256]{1,0:T(8,128)(2,1)}, u32[]{:S(2)}) copy-start(bf16[768,256]{1,0:T(8,128)(2,1)} %constant.27.clone.low_ref) | copy-start | bytes 1179652
  58.4 48.6 %copy-start.7 = (bf16[768,256]{1,0:T(8,128)(2,1)S(1)}, bf16[768,256]{1,0:T(8,128)(2,1)}, u32[]{:S(2)}) copy-start(bf16[768,256]{1,0:T(8,128)(2,1)} %constant.26.clone.high_ref) | copy-start | bytes 1179652
  59.7 63.4 %copy-start.4 = (bf16[256,768]{1,0:T(8,128)(2,1)S(1)}, bf16[256,768]{1,0:T(8,128)(2,1)}, u32[]{:S(2)}) copy-start(bf16[256,768]{1,0:T(8,128)(2,1)} %constant.29.clone.low_ref) | copy-start | bytes 1179652
  59.7 63.4 %copy-start.5 = (bf16[256,768]{1,0:T(8,128)(2,1)S(1)}, bf16[256,768]{1,0:T(8,128)(2,1)}, u32[]{:S(2)}) copy-start(bf16[256,768]{1,0:T(8,128)(2,1)} %constant.28.clone.high_ref) | copy-start | bytes 1179652

commit v5 on v3

--- a/solution.py
+++ b/solution.py
@@ -17,6 +17,7 @@
 GROUP = 16
 GX_ORDER = [2 * z + x_lo for x_lo in range(2) for z in range(8)]
 GY_ORDER = [8 * x_hi + 2 * y + core for core in (1, 0) for y in (0, 2, 1, 3) for x_hi in range(2)]
+THIRD_ORDER = [chip + core for core in (1, 0) for chip in (6, 10, 4, 8, 14, 12, 0, 2)]
 LAST_ORDER = [3, 14, 7, 9, 13, 11, 4, 5, 12, 8, 1, 0, 15, 6, 2, 10]
 ENDS = {
     axis: [[order.index(device + 8 * end) for device in range(8)] for end in range(2)]
@@ -86,7 +87,9 @@
 def z_table():
     ops = np.stack([circulant_table(NZ, power) for power in range(3)])
     ops = ops.reshape(3, GROUP, NZ // GROUP, NZ).transpose(1, 0, 2, 3)[GX_ORDER].reshape(3 * NZ, NZ)
-    return [np.kron(part, np.eye(2, dtype=ml_dtypes.bfloat16)) for part in split(ops, 1)]
+    blocks = [GY_ORDER.index(device) for device in THIRD_ORDER]
+    parts = [part.reshape(3 * NZ, GROUP, -1)[:, blocks].reshape(3 * NZ, NZ) for part in split(ops, 1)]
+    return [np.kron(part, np.eye(2, dtype=ml_dtypes.bfloat16)) for part in parts]
 
 
 def y_table():
@@ -98,7 +101,7 @@
 
 def x_table():
     ops = np.concatenate([inverse_table(NX, MX, power).T for power in range(3)], axis=1)
-    blocks = [GY_ORDER.index(device) for device in LAST_ORDER]
+    blocks = [THIRD_ORDER.index(device) for device in LAST_ORDER]
     return ops.reshape(GROUP, -1, 3 * MX)[blocks].reshape(MX, 3 * MX)
 
 
@@ -259,7 +262,7 @@
         scratch=(pltpu.VMEM((2, 64, 128), F32),),
     )
 
-    lines = exchange(lines, "gy", GY_ORDER).reshape(GROUP * 8, 128)
+    lines = exchange(lines, "gy", THIRD_ORDER).reshape(GROUP * 8, 128)
     lines = call(along_z, (6 * NZ, 128), (lines, *z_table()))
 
     lines = exchange(lines.reshape(GROUP, 24, 128), "gx", GX_ORDER).reshape(6 * NZ, 128)

time: 125 us -> 126 us (level)
  no operation moved by 1% of the time
where the time goes in v5:
time: 126 us
  blocking collectives  121 us (96%)
  Pallas kernels  4.25 us (3%)
    all_to_all x5, blocking collectives, exchange(): lax.all_to_all(value, axis, split_axis=0, concat_axis=0, tiled=True, axis...  121 us
    pallas_call x5, Pallas kernels, call(): pl.pallas_call(kernel, out_shape=jax.ShapeDtypeStruct(out_shape, F32), in...  4.25 us

profile of v5, /device:TPU:1, one launch (start us, length us, event | category | flops | bytes accessed | tf_op | source)
XLA Modules:
  0.0 125.6 jit_solution(14803641091949245981)
XLA Ops:
  0.0 0.0 copy-start.2
  0.0 0.0 copy-start.3
  0.0 58.4 %all_to_all.25 = f32[16,512,128]{2,1,0:T(8,128)S(1)} all-to-all(f32[16,512,128]{2,1,0:T(8,128)} %bitcast.15), channel_id=1, replica_groups={{1,9,5,13,3,11,7,15,0,8,4,12,2,10,6,14},{17,25,21,29,19,27,23,31,16,24,..., dimensions={0} | all-to-all | bytes 8388608 | tf_op jit(solution)/shard_map/all_to_all | solution.py:244
  58.4 0.0 copy-start
  58.4 0.0 copy-start.1
  58.4 0.0 copy-done.2
  58.4 0.0 copy-done.3
  58.4 0.0 copy-start.8
  58.4 0.0 copy-start.9
  58.4 0.0 copy-start.6
  58.4 0.0 copy-start.7
  58.5 1.3 %shard_map.109 = f32[16,4,16,128]{3,2,1,0:T(8,128)S(1)} custom-call(f32[16,4,128,128]{3,2,1,0:T(8,128)S(1)} %bitcast.8, bf16[2,128,1024]{2,1,0:T(8,128)(2,1)S(1)} %copy-done.3, bf16[2,128,1024]{2,1,0:T(8,128)(2,1)S(1)} %copy-done.2), custom_call_target="tpu_custom_call" | custom-call | tf_op jit(solution)/shard_map/pallas_call | solution.py:233
  59.8 0.0 copy-start.4
  59.8 0.0 copy-start.5
  59.8 21.5 %all_to_all.26.v_ref = f32[16,64,128]{2,1,0:T(8,128)S(1)} all-to-all(f32[16,64,128]{2,1,0:T(8,128)S(1)} %bitcast.9), channel_id=1, replica_groups={{0,32,64,96,128,160,192,224,16,48,80,112,144,176,208,240},{1,33,65,97,1..., dimensions={0} | all-to-all | bytes 1048576 | tf_op jit(solution)/shard_map/all_to_all | solution.py:244
  81.3 0.0 copy-done
  81.3 0.0 copy-done.1
  81.3 0.6 shard_map.110
  81.9 13.5 %all_to_all.27 = f32[16,8,128]{2,1,0:T(8,128)S(1)} all-to-all(f32[16,8,128]{2,1,0:T(8,128)S(1)} %shard_map.110), channel_id=1, replica_groups={{7,11,5,9,15,13,1,3,6,10,4,8,14,12,0,2},{23,27,21,25,31,29,17,19,22,26,..., dimensions={0} | all-to-all | bytes 131072 | tf_op jit(solution)/shard_map/all_to_all | solution.py:244
  95.4 0.0 copy-done.8
  95.4 0.0 copy-done.9
  95.4 0.2 shard_map.111
  95.6 11.5 %all_to_all.28 = f32[16,24,128]{2,1,0:T(8,128)S(1)} all-to-all(f32[16,24,128]{2,1,0:T(8,128)S(1)} %bitcast.12), channel_id=1, replica_groups={{0,32,64,96,128,160,192,224,16,48,80,112,144,176,208,240},{1,33,65,97,1..., dimensions={0} | all-to-all | bytes 393216 | tf_op jit(solution)/shard_map/all_to_all | solution.py:244
  107.2 0.0 copy-done.6
  107.2 0.0 copy-done.7
  107.2 0.7 shard_map.112
  107.9 16.3 %all_to_all.29 = f32[16,48,128]{2,1,0:T(8,128)S(1)} all-to-all(f32[16,48,128]{2,1,0:T(8,128)S(1)} %bitcast.11), channel_id=1, replica_groups={{3,14,7,9,13,11,4,5,12,8,1,0,15,6,2,10},{19,30,23,25,29,27,20,21,28,24,..., dimensions={0} | all-to-all | bytes 786432 | tf_op jit(solution)/shard_map/all_to_all | solution.py:244
  124.2 0.0 copy-done.4
  124.2 0.0 copy-done.5
  124.2 1.4 %shard_map.113 = f32[9,4,16,256]{3,2,1,0:T(8,128)} custom-call(f32[16,3,16,128]{3,2,1,0:T(8,128)S(1)} %bitcast.10, bf16[256,768]{1,0:T(8,128)(2,1)S(1)} %copy-done.5, bf16[256,768]{1,0:T(8,128)(2,1)S(1)} %copy-done.4), custom_call_target="tpu_custom_call" | custom-call | tf_op jit(solution)/shard_map/pallas_call | solution.py:233
Async XLA Ops:
  0.0 58.4 %copy-start.2 = (bf16[2,128,1024]{2,1,0:T(8,128)(2,1)S(1)}, bf16[2,128,1024]{2,1,0:T(8,128)(2,1)}, u32[]{:S(2)}) copy-start(bf16[2,128,1024]{2,1,0:T(8,128)(2,1)} %constant.21.clone.low_ref) | copy-start | bytes 1572868
  0.0 58.4 %copy-start.3 = (bf16[2,128,1024]{2,1,0:T(8,128)(2,1)S(1)}, bf16[2,128,1024]{2,1,0:T(8,128)(2,1)}, u32[]{:S(2)}) copy-start(bf16[2,128,1024]{2,1,0:T(8,128)(2,1)} %constant.20.clone.high_ref) | copy-start | bytes 1572868
  58.4 22.9 %copy-start = (bf16[2,1024,128]{2,1,0:T(8,128)(2,1)S(1)}, bf16[2,1024,128]{2,1,0:T(8,128)(2,1)}, u32[]{:S(2)}) copy-start(bf16[2,1024,128]{2,1,0:T(8,128)(2,1)} %constant.23.clone.low_ref) | copy-start | bytes 1572868
  58.4 22.9 %copy-start.1 = (bf16[2,1024,128]{2,1,0:T(8,128)(2,1)S(1)}, bf16[2,1024,128]{2,1,0:T(8,128)(2,1)}, u32[]{:S(2)}) copy-start(bf16[2,1024,128]{2,1,0:T(8,128)(2,1)} %constant.22.clone.high_ref) | copy-start | bytes 1572868
  58.4 37.0 %copy-start.8 = (bf16[384,128]{1,0:T(8,128)(2,1)S(1)}, bf16[384,128]{1,0:T(8,128)(2,1)}, u32[]{:S(2)}) copy-start(bf16[384,128]{1,0:T(8,128)(2,1)} %constant.25.clone.low_ref) | copy-start | bytes 294916
  58.4 37.0 %copy-start.9 = (bf16[384,128]{1,0:T(8,128)(2,1)S(1)}, bf16[384,128]{1,0:T(8,128)(2,1)}, u32[]{:S(2)}) copy-start(bf16[384,128]{1,0:T(8,128)(2,1)} %constant.24.clone.high_ref) | copy-start | bytes 294916
  58.4 48.7 %copy-start.6 = (bf16[768,256]{1,0:T(8,128)(2,1)S(1)}, bf16[768,256]{1,0:T(8,128)(2,1)}, u32[]{:S(2)}) copy-start(bf16[768,256]{1,0:T(8,128)(2,1)} %constant.27.clone.low_ref) | copy-start | bytes 1179652
  58.4 48.7 %copy-start.7 = (bf16[768,256]{1,0:T(8,128)(2,1)S(1)}, bf16[768,256]{1,0:T(8,128)(2,1)}, u32[]{:S(2)}) copy-start(bf16[768,256]{1,0:T(8,128)(2,1)} %constant.26.clone.high_ref) | copy-start | bytes 1179652
  59.8 64.4 %copy-start.4 = (bf16[256,768]{1,0:T(8,128)(2,1)S(1)}, bf16[256,768]{1,0:T(8,128)(2,1)}, u32[]{:S(2)}) copy-start(bf16[256,768]{1,0:T(8,128)(2,1)} %constant.29.clone.low_ref) | copy-start | bytes 1179652
  59.8 64.4 %copy-start.5 = (bf16[256,768]{1,0:T(8,128)(2,1)S(1)}, bf16[256,768]{1,0:T(8,128)(2,1)}, u32[]{:S(2)}) copy-start(bf16[256,768]{1,0:T(8,128)(2,1)} %constant.28.clone.high_ref) | copy-start | bytes 1179652

commit v6 on v3

--- a/solution.py
+++ b/solution.py
@@ -17,7 +17,6 @@
 GROUP = 16
 GX_ORDER = [2 * z + x_lo for x_lo in range(2) for z in range(8)]
 GY_ORDER = [8 * x_hi + 2 * y + core for core in (1, 0) for y in (0, 2, 1, 3) for x_hi in range(2)]
-LAST_ORDER = [3, 14, 7, 9, 13, 11, 4, 5, 12, 8, 1, 0, 15, 6, 2, 10]
 ENDS = {
     axis: [[order.index(device + 8 * end) for device in range(8)] for end in range(2)]
     for axis, order in (("gx", GX_ORDER), ("gy", GY_ORDER))
@@ -91,15 +90,13 @@
 
 def y_table():
     ops = np.stack([inverse_table(NY, MY, power) for power in range(3)])
-    ops = ops.reshape(3, GROUP, -1, MY)[:, LAST_ORDER]
+    ops = ops.reshape(3, GROUP, -1, MY)[:, GY_ORDER]
     ops = ops.reshape(3 * MY, GROUP, 2, 8).transpose(0, 3, 2, 1)
     return ops.reshape(3 * MY, MY)
 
 
 def x_table():
-    ops = np.concatenate([inverse_table(NX, MX, power).T for power in range(3)], axis=1)
-    blocks = [GY_ORDER.index(device) for device in LAST_ORDER]
-    return ops.reshape(GROUP, -1, 3 * MX)[blocks].reshape(MX, 3 * MX)
+    return np.concatenate([inverse_table(NX, MX, power).T for power in range(3)], axis=1)
 
 
 def split_value(value):
@@ -265,7 +262,7 @@
     lines = exchange(lines.reshape(GROUP, 24, 128), "gx", GX_ORDER).reshape(6 * NZ, 128)
     lines = call(inverse_y, (GROUP, 3, GROUP, 128), (lines, *split(y_table())))
 
-    lines = exchange(lines.reshape(GROUP, 48, 128), "gy", LAST_ORDER).reshape(GROUP, 3, GROUP, 128)
+    lines = exchange(lines.reshape(GROUP, 48, 128), "gy", GY_ORDER).reshape(GROUP, 3, GROUP, 128)
     return call(
         inverse_x,
         (9, 4, GROUP, MX),

time: 125 us -> 124 us (level)
  no operation moved by 1% of the time
where the time goes in v6:
time: 124 us
  blocking collectives  120 us (97%)
  Pallas kernels  4.25 us (3%)
    all_to_all x5, blocking collectives, exchange(): lax.all_to_all(value, axis, split_axis=0, concat_axis=0, tiled=True, axis...  120 us
    pallas_call x5, Pallas kernels, call(): pl.pallas_call(kernel, out_shape=jax.ShapeDtypeStruct(out_shape, F32), in...  4.25 us

profile of v6, /device:TPU:1, one launch (start us, length us, event | category | flops | bytes accessed | tf_op | source)
XLA Modules:
  0.0 124.0 jit_solution(1696417948132255041)
XLA Ops:
  0.0 0.0 copy-start.2
  0.0 0.0 copy-start.3
  0.0 58.4 %all_to_all.25 = f32[16,512,128]{2,1,0:T(8,128)S(1)} all-to-all(f32[16,512,128]{2,1,0:T(8,128)} %bitcast.15), channel_id=1, replica_groups={{1,9,5,13,3,11,7,15,0,8,4,12,2,10,6,14},{17,25,21,29,19,27,23,31,16,24,..., dimensions={0} | all-to-all | bytes 8388608 | tf_op jit(solution)/shard_map/all_to_all | solution.py:238
  58.4 0.0 copy-start
  58.4 0.0 copy-start.1
  58.4 0.0 copy-done.2
  58.4 0.0 copy-done.3
  58.4 0.0 copy-start.8
  58.4 0.0 copy-start.9
  58.4 0.0 copy-start.6
  58.4 0.0 copy-start.7
  58.5 1.3 %shard_map.109 = f32[16,4,16,128]{3,2,1,0:T(8,128)S(1)} custom-call(f32[16,4,128,128]{3,2,1,0:T(8,128)S(1)} %bitcast.8, bf16[2,128,1024]{2,1,0:T(8,128)(2,1)S(1)} %copy-done.3, bf16[2,128,1024]{2,1,0:T(8,128)(2,1)S(1)} %copy-done.2), custom_call_target="tpu_custom_call" | custom-call | tf_op jit(solution)/shard_map/pallas_call | solution.py:227
  59.8 0.0 copy-start.4
  59.8 0.0 copy-start.5
  59.8 21.5 %all_to_all.26.v_ref = f32[16,64,128]{2,1,0:T(8,128)S(1)} all-to-all(f32[16,64,128]{2,1,0:T(8,128)S(1)} %bitcast.9), channel_id=1, replica_groups={{0,32,64,96,128,160,192,224,16,48,80,112,144,176,208,240},{1,33,65,97,1..., dimensions={0} | all-to-all | bytes 1048576 | tf_op jit(solution)/shard_map/all_to_all | solution.py:238
  81.3 0.0 copy-done
  81.3 0.0 copy-done.1
  81.3 0.6 shard_map.110
  81.9 13.5 %all_to_all.27 = f32[16,8,128]{2,1,0:T(8,128)S(1)} all-to-all(f32[16,8,128]{2,1,0:T(8,128)S(1)} %shard_map.110), channel_id=1, replica_groups={{1,9,5,13,3,11,7,15,0,8,4,12,2,10,6,14},{17,25,21,29,19,27,23,31,16,24,..., dimensions={0} | all-to-all | bytes 131072 | tf_op jit(solution)/shard_map/all_to_all | solution.py:238
  95.4 0.0 copy-done.8
  95.4 0.0 copy-done.9
  95.4 0.2 shard_map.111
  95.6 11.6 %all_to_all.28 = f32[16,24,128]{2,1,0:T(8,128)S(1)} all-to-all(f32[16,24,128]{2,1,0:T(8,128)S(1)} %bitcast.12), channel_id=1, replica_groups={{0,32,64,96,128,160,192,224,16,48,80,112,144,176,208,240},{1,33,65,97,1..., dimensions={0} | all-to-all | bytes 393216 | tf_op jit(solution)/shard_map/all_to_all | solution.py:238
  107.2 0.0 copy-done.6
  107.2 0.0 copy-done.7
  107.2 0.7 shard_map.112
  107.9 14.6 %all_to_all.29 = f32[16,48,128]{2,1,0:T(8,128)S(1)} all-to-all(f32[16,48,128]{2,1,0:T(8,128)S(1)} %bitcast.11), channel_id=1, replica_groups={{1,9,5,13,3,11,7,15,0,8,4,12,2,10,6,14},{17,25,21,29,19,27,23,31,16,24,..., dimensions={0} | all-to-all | bytes 786432 | tf_op jit(solution)/shard_map/all_to_all | solution.py:238
  122.5 0.0 copy-done.4
  122.5 0.0 copy-done.5
  122.5 1.4 %shard_map.113 = f32[9,4,16,256]{3,2,1,0:T(8,128)} custom-call(f32[16,3,16,128]{3,2,1,0:T(8,128)S(1)} %bitcast.10, bf16[256,768]{1,0:T(8,128)(2,1)S(1)} %copy-done.5, bf16[256,768]{1,0:T(8,128)(2,1)S(1)} %copy-done.4), custom_call_target="tpu_custom_call" | custom-call | tf_op jit(solution)/shard_map/pallas_call | solution.py:227
Async XLA Ops:
  0.0 58.4 %copy-start.2 = (bf16[2,128,1024]{2,1,0:T(8,128)(2,1)S(1)}, bf16[2,128,1024]{2,1,0:T(8,128)(2,1)}, u32[]{:S(2)}) copy-start(bf16[2,128,1024]{2,1,0:T(8,128)(2,1)} %constant.21.clone.low_ref) | copy-start | bytes 1572868
  0.0 58.4 %copy-start.3 = (bf16[2,128,1024]{2,1,0:T(8,128)(2,1)S(1)}, bf16[2,128,1024]{2,1,0:T(8,128)(2,1)}, u32[]{:S(2)}) copy-start(bf16[2,128,1024]{2,1,0:T(8,128)(2,1)} %constant.20.clone.high_ref) | copy-start | bytes 1572868
  58.4 22.9 %copy-start = (bf16[2,1024,128]{2,1,0:T(8,128)(2,1)S(1)}, bf16[2,1024,128]{2,1,0:T(8,128)(2,1)}, u32[]{:S(2)}) copy-start(bf16[2,1024,128]{2,1,0:T(8,128)(2,1)} %constant.23.clone.low_ref) | copy-start | bytes 1572868
  58.4 22.9 %copy-start.1 = (bf16[2,1024,128]{2,1,0:T(8,128)(2,1)S(1)}, bf16[2,1024,128]{2,1,0:T(8,128)(2,1)}, u32[]{:S(2)}) copy-start(bf16[2,1024,128]{2,1,0:T(8,128)(2,1)} %constant.22.clone.high_ref) | copy-start | bytes 1572868
  58.4 37.0 %copy-start.8 = (bf16[384,128]{1,0:T(8,128)(2,1)S(1)}, bf16[384,128]{1,0:T(8,128)(2,1)}, u32[]{:S(2)}) copy-start(bf16[384,128]{1,0:T(8,128)(2,1)} %constant.25.clone.low_ref) | copy-start | bytes 294916
  58.4 37.0 %copy-start.9 = (bf16[384,128]{1,0:T(8,128)(2,1)S(1)}, bf16[384,128]{1,0:T(8,128)(2,1)}, u32[]{:S(2)}) copy-start(bf16[384,128]{1,0:T(8,128)(2,1)} %constant.24.clone.high_ref) | copy-start | bytes 294916
  58.4 48.8 %copy-start.6 = (bf16[768,256]{1,0:T(8,128)(2,1)S(1)}, bf16[768,256]{1,0:T(8,128)(2,1)}, u32[]{:S(2)}) copy-start(bf16[768,256]{1,0:T(8,128)(2,1)} %constant.27.clone.low_ref) | copy-start | bytes 1179652
  58.4 48.7 %copy-start.7 = (bf16[768,256]{1,0:T(8,128)(2,1)S(1)}, bf16[768,256]{1,0:T(8,128)(2,1)}, u32[]{:S(2)}) copy-start(bf16[768,256]{1,0:T(8,128)(2,1)} %constant.26.clone.high_ref) | copy-start | bytes 1179652
  59.8 62.8 %copy-start.4 = (bf16[256,768]{1,0:T(8,128)(2,1)S(1)}, bf16[256,768]{1,0:T(8,128)(2,1)}, u32[]{:S(2)}) copy-start(bf16[256,768]{1,0:T(8,128)(2,1)} %constant.29.clone.low_ref) | copy-start | bytes 1179652
  59.8 62.7 %copy-start.5 = (bf16[256,768]{1,0:T(8,128)(2,1)S(1)}, bf16[256,768]{1,0:T(8,128)(2,1)}, u32[]{:S(2)}) copy-start(bf16[256,768]{1,0:T(8,128)(2,1)} %constant.28.clone.high_ref) | copy-start | bytes 1179652

commit v7 on v6

--- a/solution.py
+++ b/solution.py
@@ -112,6 +112,12 @@
     return dot(a[0], b[0]) + dot(a[0], b[1]) + dot(a[1], b[0])
 
 
+def stacked_dot3(a, b):
+    rows = a[0].shape[0]
+    both = dot(jnp.concatenate(a, axis=0), b[0])
+    return both[:rows] + both[rows:] + dot(a[0], b[1])
+
+
 def swap_blocks(arrays):
     block = lax.broadcasted_iota(jnp.int32, arrays[0].shape, 1) // 16
     arrays = list(arrays)
@@ -140,7 +146,7 @@
         for end in ENDS["gy"]
     ]
     for parity, lines in enumerate(fold(*ends)):
-        product = dot3((high_ref[parity], low_ref[parity]), lines)
+        product = stacked_dot3((high_ref[parity], low_ref[parity]), lines)
         for z in range(planes):
             piece = product[:, 128 * z : 128 * (z + 1)].reshape(GROUP // 2, GROUP, 128)
             out_ref[8 * parity : 8 * parity + 8, z] = piece

time: 124 us -> 124 us (level)
  no operation moved by 1% of the time
where the time goes in v7:
time: 124 us
  blocking collectives  120 us (97%)
  Pallas kernels  4.14 us (3%)
    all_to_all x5, blocking collectives, exchange(): lax.all_to_all(value, axis, split_axis=0, concat_axis=0, tiled=True, axis...  120 us
    pallas_call x5, Pallas kernels, call(): pl.pallas_call(kernel, out_shape=jax.ShapeDtypeStruct(out_shape, F32), in...  4.14 us

profile of v7, /device:TPU:1, one launch (start us, length us, event | category | flops | bytes accessed | tf_op | source)
XLA Modules:
  0.0 123.8 jit_solution(13847810858875260601)
XLA Ops:
  0.0 0.0 copy-start.2
  0.0 0.0 copy-start.3
  0.0 58.4 %all_to_all.25 = f32[16,512,128]{2,1,0:T(8,128)S(1)} all-to-all(f32[16,512,128]{2,1,0:T(8,128)} %bitcast.15), channel_id=1, replica_groups={{1,9,5,13,3,11,7,15,0,8,4,12,2,10,6,14},{17,25,21,29,19,27,23,31,16,24,..., dimensions={0} | all-to-all | bytes 8388608 | tf_op jit(solution)/shard_map/all_to_all | solution.py:244
  58.4 0.0 copy-start
  58.4 0.0 copy-start.1
  58.4 0.0 copy-done.2
  58.4 0.0 copy-done.3
  58.4 0.0 copy-start.8
  58.4 0.0 copy-start.9
  58.4 0.0 copy-start.6
  58.4 0.0 copy-start.7
  58.5 1.2 shard_map.109
  59.7 0.0 copy-start.4
  59.7 0.0 copy-start.5
  59.7 21.5 %all_to_all.26.v_ref = f32[16,64,128]{2,1,0:T(8,128)S(1)} all-to-all(f32[16,64,128]{2,1,0:T(8,128)S(1)} %bitcast.9), channel_id=1, replica_groups={{0,32,64,96,128,160,192,224,16,48,80,112,144,176,208,240},{1,33,65,97,1..., dimensions={0} | all-to-all | bytes 1048576 | tf_op jit(solution)/shard_map/all_to_all | solution.py:244
  81.2 0.0 copy-done
  81.2 0.0 copy-done.1
  81.2 0.6 shard_map.110
  81.7 13.5 %all_to_all.27 = f32[16,8,128]{2,1,0:T(8,128)S(1)} all-to-all(f32[16,8,128]{2,1,0:T(8,128)S(1)} %shard_map.110), channel_id=1, replica_groups={{1,9,5,13,3,11,7,15,0,8,4,12,2,10,6,14},{17,25,21,29,19,27,23,31,16,24,..., dimensions={0} | all-to-all | bytes 131072 | tf_op jit(solution)/shard_map/all_to_all | solution.py:244
  95.2 0.0 copy-done.8
  95.2 0.0 copy-done.9
  95.2 0.2 shard_map.111
  95.5 11.6 %all_to_all.28 = f32[16,24,128]{2,1,0:T(8,128)S(1)} all-to-all(f32[16,24,128]{2,1,0:T(8,128)S(1)} %bitcast.12), channel_id=1, replica_groups={{0,32,64,96,128,160,192,224,16,48,80,112,144,176,208,240},{1,33,65,97,1..., dimensions={0} | all-to-all | bytes 393216 | tf_op jit(solution)/shard_map/all_to_all | solution.py:244
  107.1 0.0 copy-done.6
  107.1 0.0 copy-done.7
  107.1 0.7 shard_map.112
  107.8 14.6 %all_to_all.29 = f32[16,48,128]{2,1,0:T(8,128)S(1)} all-to-all(f32[16,48,128]{2,1,0:T(8,128)S(1)} %bitcast.11), channel_id=1, replica_groups={{1,9,5,13,3,11,7,15,0,8,4,12,2,10,6,14},{17,25,21,29,19,27,23,31,16,24,..., dimensions={0} | all-to-all | bytes 786432 | tf_op jit(solution)/shard_map/all_to_all | solution.py:244
  122.4 0.0 copy-done.4
  122.4 0.0 copy-done.5
  122.4 1.4 %shard_map.113 = f32[9,4,16,256]{3,2,1,0:T(8,128)} custom-call(f32[16,3,16,128]{3,2,1,0:T(8,128)S(1)} %bitcast.10, bf16[256,768]{1,0:T(8,128)(2,1)S(1)} %copy-done.5, bf16[256,768]{1,0:T(8,128)(2,1)S(1)} %copy-done.4), custom_call_target="tpu_custom_call" | custom-call | tf_op jit(solution)/shard_map/pallas_call | solution.py:233
Async XLA Ops:
  0.0 58.4 %copy-start.2 = (bf16[2,128,1024]{2,1,0:T(8,128)(2,1)S(1)}, bf16[2,128,1024]{2,1,0:T(8,128)(2,1)}, u32[]{:S(2)}) copy-start(bf16[2,128,1024]{2,1,0:T(8,128)(2,1)} %constant.21.clone.low_ref) | copy-start | bytes 1572868
  0.0 58.4 %copy-start.3 = (bf16[2,128,1024]{2,1,0:T(8,128)(2,1)S(1)}, bf16[2,128,1024]{2,1,0:T(8,128)(2,1)}, u32[]{:S(2)}) copy-start(bf16[2,128,1024]{2,1,0:T(8,128)(2,1)} %constant.20.clone.high_ref) | copy-start | bytes 1572868
  58.4 22.8 %copy-start = (bf16[2,1024,128]{2,1,0:T(8,128)(2,1)S(1)}, bf16[2,1024,128]{2,1,0:T(8,128)(2,1)}, u32[]{:S(2)}) copy-start(bf16[2,1024,128]{2,1,0:T(8,128)(2,1)} %constant.23.clone.low_ref) | copy-start | bytes 1572868
  58.4 22.8 %copy-start.1 = (bf16[2,1024,128]{2,1,0:T(8,128)(2,1)S(1)}, bf16[2,1024,128]{2,1,0:T(8,128)(2,1)}, u32[]{:S(2)}) copy-start(bf16[2,1024,128]{2,1,0:T(8,128)(2,1)} %constant.22.clone.high_ref) | copy-start | bytes 1572868
  58.4 36.8 %copy-start.8 = (bf16[384,128]{1,0:T(8,128)(2,1)S(1)}, bf16[384,128]{1,0:T(8,128)(2,1)}, u32[]{:S(2)}) copy-start(bf16[384,128]{1,0:T(8,128)(2,1)} %constant.25.clone.low_ref) | copy-start | bytes 294916
  58.4 36.8 %copy-start.9 = (bf16[384,128]{1,0:T(8,128)(2,1)S(1)}, bf16[384,128]{1,0:T(8,128)(2,1)}, u32[]{:S(2)}) copy-start(bf16[384,128]{1,0:T(8,128)(2,1)} %constant.24.clone.high_ref) | copy-start | bytes 294916
  58.4 48.6 %copy-start.6 = (bf16[768,256]{1,0:T(8,128)(2,1)S(1)}, bf16[768,256]{1,0:T(8,128)(2,1)}, u32[]{:S(2)}) copy-start(bf16[768,256]{1,0:T(8,128)(2,1)} %constant.27.clone.low_ref) | copy-start | bytes 1179652
  58.4 48.6 %copy-start.7 = (bf16[768,256]{1,0:T(8,128)(2,1)S(1)}, bf16[768,256]{1,0:T(8,128)(2,1)}, u32[]{:S(2)}) copy-start(bf16[768,256]{1,0:T(8,128)(2,1)} %constant.26.clone.high_ref) | copy-start | bytes 1179652
  59.7 62.7 %copy-start.4 = (bf16[256,768]{1,0:T(8,128)(2,1)S(1)}, bf16[256,768]{1,0:T(8,128)(2,1)}, u32[]{:S(2)}) copy-start(bf16[256,768]{1,0:T(8,128)(2,1)} %constant.29.clone.low_ref) | copy-start | bytes 1179652
  59.7 62.7 %copy-start.5 = (bf16[256,768]{1,0:T(8,128)(2,1)S(1)}, bf16[256,768]{1,0:T(8,128)(2,1)}, u32[]{:S(2)}) copy-start(bf16[256,768]{1,0:T(8,128)(2,1)} %constant.28.clone.high_ref) | copy-start | bytes 1179652

commit v8 on v6

--- a/solution.py
+++ b/solution.py
@@ -15,7 +15,7 @@
 MX = 256
 MY = 256
 GROUP = 16
-GX_ORDER = [2 * z + x_lo for x_lo in range(2) for z in range(8)]
+GX_ORDER = [2 * z + x_lo for x_lo in range(2) for z in (0, 2, 4, 6, 1, 3, 5, 7)]
 GY_ORDER = [8 * x_hi + 2 * y + core for core in (1, 0) for y in (0, 2, 1, 3) for x_hi in range(2)]
 ENDS = {
     axis: [[order.index(device + 8 * end) for device in range(8)] for end in range(2)]

time: 124 us -> 125 us (level)
  no operation moved by 1% of the time
where the time goes in v8:
time: 125 us
  blocking collectives  120 us (96%)
  Pallas kernels  4.25 us (3%)
    all_to_all x5, blocking collectives, exchange(): lax.all_to_all(value, axis, split_axis=0, concat_axis=0, tiled=True, axis...  120 us
    pallas_call x5, Pallas kernels, call(): pl.pallas_call(kernel, out_shape=jax.ShapeDtypeStruct(out_shape, F32), in...  4.25 us

profile of v8, /device:TPU:1, one launch (start us, length us, event | category | flops | bytes accessed | tf_op | source)
XLA Modules:
  0.0 124.7 jit_solution(741404690397082960)
XLA Ops:
  0.0 0.0 copy-start.2
  0.0 0.0 copy-start.3
  0.0 58.4 %all_to_all.25 = f32[16,512,128]{2,1,0:T(8,128)S(1)} all-to-all(f32[16,512,128]{2,1,0:T(8,128)} %bitcast.15), channel_id=1, replica_groups={{1,9,5,13,3,11,7,15,0,8,4,12,2,10,6,14},{17,25,21,29,19,27,23,31,16,24,..., dimensions={0} | all-to-all | bytes 8388608 | tf_op jit(solution)/shard_map/all_to_all | solution.py:238
  58.4 0.0 copy-start
  58.4 0.0 copy-start.1
  58.4 0.0 copy-done.2
  58.4 0.0 copy-done.3
  58.4 0.0 copy-start.8
  58.4 0.0 copy-start.9
  58.4 0.0 copy-start.6
  58.4 0.0 copy-start.7
  58.5 1.3 %shard_map.109 = f32[16,4,16,128]{3,2,1,0:T(8,128)S(1)} custom-call(f32[16,4,128,128]{3,2,1,0:T(8,128)S(1)} %bitcast.8, bf16[2,128,1024]{2,1,0:T(8,128)(2,1)S(1)} %copy-done.3, bf16[2,128,1024]{2,1,0:T(8,128)(2,1)S(1)} %copy-done.2), custom_call_target="tpu_custom_call" | custom-call | tf_op jit(solution)/shard_map/pallas_call | solution.py:227
  59.8 0.0 copy-start.4
  59.8 0.0 copy-start.5
  59.8 20.6 %all_to_all.26.v_ref = f32[16,64,128]{2,1,0:T(8,128)S(1)} all-to-all(f32[16,64,128]{2,1,0:T(8,128)S(1)} %bitcast.9), channel_id=1, replica_groups={{0,64,128,192,32,96,160,224,16,80,144,208,48,112,176,240},{1,65,129,193..., dimensions={0} | all-to-all | bytes 1048576 | tf_op jit(solution)/shard_map/all_to_all | solution.py:238
  80.4 0.0 copy-done
  80.4 0.0 copy-done.1
  80.5 0.6 shard_map.110
  81.0 14.7 %all_to_all.27 = f32[16,8,128]{2,1,0:T(8,128)S(1)} all-to-all(f32[16,8,128]{2,1,0:T(8,128)S(1)} %shard_map.110), channel_id=1, replica_groups={{1,9,5,13,3,11,7,15,0,8,4,12,2,10,6,14},{17,25,21,29,19,27,23,31,16,24,..., dimensions={0} | all-to-all | bytes 131072 | tf_op jit(solution)/shard_map/all_to_all | solution.py:238
  95.7 0.0 copy-done.8
  95.7 0.0 copy-done.9
  95.7 0.2 shard_map.111
  95.9 11.4 %all_to_all.28 = f32[16,24,128]{2,1,0:T(8,128)S(1)} all-to-all(f32[16,24,128]{2,1,0:T(8,128)S(1)} %bitcast.12), channel_id=1, replica_groups={{0,64,128,192,32,96,160,224,16,80,144,208,48,112,176,240},{1,65,129,193..., dimensions={0} | all-to-all | bytes 393216 | tf_op jit(solution)/shard_map/all_to_all | solution.py:238
  107.4 0.0 copy-done.6
  107.4 0.0 copy-done.7
  107.4 0.7 shard_map.112
  108.1 15.2 %all_to_all.29 = f32[16,48,128]{2,1,0:T(8,128)S(1)} all-to-all(f32[16,48,128]{2,1,0:T(8,128)S(1)} %bitcast.11), channel_id=1, replica_groups={{1,9,5,13,3,11,7,15,0,8,4,12,2,10,6,14},{17,25,21,29,19,27,23,31,16,24,..., dimensions={0} | all-to-all | bytes 786432 | tf_op jit(solution)/shard_map/all_to_all | solution.py:238
  123.3 0.0 copy-done.4
  123.3 0.0 copy-done.5
  123.3 1.4 %shard_map.113 = f32[9,4,16,256]{3,2,1,0:T(8,128)} custom-call(f32[16,3,16,128]{3,2,1,0:T(8,128)S(1)} %bitcast.10, bf16[256,768]{1,0:T(8,128)(2,1)S(1)} %copy-done.5, bf16[256,768]{1,0:T(8,128)(2,1)S(1)} %copy-done.4), custom_call_target="tpu_custom_call" | custom-call | tf_op jit(solution)/shard_map/pallas_call | solution.py:227
Async XLA Ops:
  0.0 58.4 %copy-start.2 = (bf16[2,128,1024]{2,1,0:T(8,128)(2,1)S(1)}, bf16[2,128,1024]{2,1,0:T(8,128)(2,1)}, u32[]{:S(2)}) copy-start(bf16[2,128,1024]{2,1,0:T(8,128)(2,1)} %constant.21.clone.low_ref) | copy-start | bytes 1572868
  0.0 58.4 %copy-start.3 = (bf16[2,128,1024]{2,1,0:T(8,128)(2,1)S(1)}, bf16[2,128,1024]{2,1,0:T(8,128)(2,1)}, u32[]{:S(2)}) copy-start(bf16[2,128,1024]{2,1,0:T(8,128)(2,1)} %constant.20.clone.high_ref) | copy-start | bytes 1572868
  58.4 22.1 %copy-start = (bf16[2,1024,128]{2,1,0:T(8,128)(2,1)S(1)}, bf16[2,1024,128]{2,1,0:T(8,128)(2,1)}, u32[]{:S(2)}) copy-start(bf16[2,1024,128]{2,1,0:T(8,128)(2,1)} %constant.23.clone.low_ref) | copy-start | bytes 1572868
  58.4 22.1 %copy-start.1 = (bf16[2,1024,128]{2,1,0:T(8,128)(2,1)S(1)}, bf16[2,1024,128]{2,1,0:T(8,128)(2,1)}, u32[]{:S(2)}) copy-start(bf16[2,1024,128]{2,1,0:T(8,128)(2,1)} %constant.22.clone.high_ref) | copy-start | bytes 1572868
  58.4 37.3 %copy-start.8 = (bf16[384,128]{1,0:T(8,128)(2,1)S(1)}, bf16[384,128]{1,0:T(8,128)(2,1)}, u32[]{:S(2)}) copy-start(bf16[384,128]{1,0:T(8,128)(2,1)} %constant.25.clone.low_ref) | copy-start | bytes 294916
  58.4 37.3 %copy-start.9 = (bf16[384,128]{1,0:T(8,128)(2,1)S(1)}, bf16[384,128]{1,0:T(8,128)(2,1)}, u32[]{:S(2)}) copy-start(bf16[384,128]{1,0:T(8,128)(2,1)} %constant.24.clone.high_ref) | copy-start | bytes 294916
  58.4 49.0 %copy-start.6 = (bf16[768,256]{1,0:T(8,128)(2,1)S(1)}, bf16[768,256]{1,0:T(8,128)(2,1)}, u32[]{:S(2)}) copy-start(bf16[768,256]{1,0:T(8,128)(2,1)} %constant.27.clone.low_ref) | copy-start | bytes 1179652
  58.4 48.9 %copy-start.7 = (bf16[768,256]{1,0:T(8,128)(2,1)S(1)}, bf16[768,256]{1,0:T(8,128)(2,1)}, u32[]{:S(2)}) copy-start(bf16[768,256]{1,0:T(8,128)(2,1)} %constant.26.clone.high_ref) | copy-start | bytes 1179652
  59.8 63.5 %copy-start.4 = (bf16[256,768]{1,0:T(8,128)(2,1)S(1)}, bf16[256,768]{1,0:T(8,128)(2,1)}, u32[]{:S(2)}) copy-start(bf16[256,768]{1,0:T(8,128)(2,1)} %constant.29.clone.low_ref) | copy-start | bytes 1179652
  59.8 63.5 %copy-start.5 = (bf16[256,768]{1,0:T(8,128)(2,1)S(1)}, bf16[256,768]{1,0:T(8,128)(2,1)}, u32[]{:S(2)}) copy-start(bf16[256,768]{1,0:T(8,128)(2,1)} %constant.28.clone.high_ref) | copy-start | bytes 1179652

commit v9 on v8

--- a/solution.py
+++ b/solution.py
@@ -15,7 +15,7 @@
 MX = 256
 MY = 256
 GROUP = 16
-GX_ORDER = [2 * z + x_lo for x_lo in range(2) for z in (0, 2, 4, 6, 1, 3, 5, 7)]
+GX_ORDER = [2 * z + x_lo for x_lo in (1, 0) for z in range(8)]
 GY_ORDER = [8 * x_hi + 2 * y + core for core in (1, 0) for y in (0, 2, 1, 3) for x_hi in range(2)]
 ENDS = {
     axis: [[order.index(device + 8 * end) for device in range(8)] for end in range(2)]

time: 125 us -> 124 us (level)
  no operation moved by 1% of the time
where the time goes in v9:
time: 124 us
  blocking collectives  120 us (97%)
  Pallas kernels  4.25 us (3%)
    all_to_all x5, blocking collectives, exchange(): lax.all_to_all(value, axis, split_axis=0, concat_axis=0, tiled=True, axis...  120 us
    pallas_call x5, Pallas kernels, call(): pl.pallas_call(kernel, out_shape=jax.ShapeDtypeStruct(out_shape, F32), in...  4.25 us

profile of v9, /device:TPU:1, one launch (start us, length us, event | category | flops | bytes accessed | tf_op | source)
XLA Modules:
  0.0 124.1 jit_solution(10144314452391257473)
XLA Ops:
  0.0 0.0 copy-start.2
  0.0 0.0 copy-start.3
  0.0 58.4 %all_to_all.25 = f32[16,512,128]{2,1,0:T(8,128)S(1)} all-to-all(f32[16,512,128]{2,1,0:T(8,128)} %bitcast.15), channel_id=1, replica_groups={{1,9,5,13,3,11,7,15,0,8,4,12,2,10,6,14},{17,25,21,29,19,27,23,31,16,24,..., dimensions={0} | all-to-all | bytes 8388608 | tf_op jit(solution)/shard_map/all_to_all | solution.py:238
  58.4 0.0 copy-start
  58.4 0.0 copy-start.1
  58.4 0.0 copy-done.2
  58.4 0.0 copy-done.3
  58.4 0.0 copy-start.8
  58.4 0.0 copy-start.9
  58.4 0.0 copy-start.6
  58.4 0.0 copy-start.7
  58.5 1.3 %shard_map.109 = f32[16,4,16,128]{3,2,1,0:T(8,128)S(1)} custom-call(f32[16,4,128,128]{3,2,1,0:T(8,128)S(1)} %bitcast.8, bf16[2,128,1024]{2,1,0:T(8,128)(2,1)S(1)} %copy-done.3, bf16[2,128,1024]{2,1,0:T(8,128)(2,1)S(1)} %copy-done.2), custom_call_target="tpu_custom_call" | custom-call | tf_op jit(solution)/shard_map/pallas_call | solution.py:227
  59.8 0.0 copy-start.4
  59.8 0.0 copy-start.5
  59.8 21.4 %all_to_all.26.v_ref = f32[16,64,128]{2,1,0:T(8,128)S(1)} all-to-all(f32[16,64,128]{2,1,0:T(8,128)S(1)} %bitcast.9), channel_id=1, replica_groups={{16,48,80,112,144,176,208,240,0,32,64,96,128,160,192,224},{17,49,81,113..., dimensions={0} | all-to-all | bytes 1048576 | tf_op jit(solution)/shard_map/all_to_all | solution.py:238
  81.2 0.0 copy-done
  81.2 0.0 copy-done.1
  81.2 0.6 shard_map.110
  81.7 13.4 %all_to_all.27 = f32[16,8,128]{2,1,0:T(8,128)S(1)} all-to-all(f32[16,8,128]{2,1,0:T(8,128)S(1)} %shard_map.110), channel_id=1, replica_groups={{1,9,5,13,3,11,7,15,0,8,4,12,2,10,6,14},{17,25,21,29,19,27,23,31,16,24,..., dimensions={0} | all-to-all | bytes 131072 | tf_op jit(solution)/shard_map/all_to_all | solution.py:238
  95.1 0.0 copy-done.8
  95.1 0.0 copy-done.9
  95.1 0.2 shard_map.111
  95.4 12.0 %all_to_all.28 = f32[16,24,128]{2,1,0:T(8,128)S(1)} all-to-all(f32[16,24,128]{2,1,0:T(8,128)S(1)} %bitcast.12), channel_id=1, replica_groups={{16,48,80,112,144,176,208,240,0,32,64,96,128,160,192,224},{17,49,81,113..., dimensions={0} | all-to-all | bytes 393216 | tf_op jit(solution)/shard_map/all_to_all | solution.py:238
  107.4 0.0 copy-done.6
  107.4 0.0 copy-done.7
  107.4 0.7 shard_map.112
  108.1 14.6 %all_to_all.29 = f32[16,48,128]{2,1,0:T(8,128)S(1)} all-to-all(f32[16,48,128]{2,1,0:T(8,128)S(1)} %bitcast.11), channel_id=1, replica_groups={{1,9,5,13,3,11,7,15,0,8,4,12,2,10,6,14},{17,25,21,29,19,27,23,31,16,24,..., dimensions={0} | all-to-all | bytes 786432 | tf_op jit(solution)/shard_map/all_to_all | solution.py:238
  122.7 0.0 copy-done.4
  122.7 0.0 copy-done.5
  122.7 1.4 %shard_map.113 = f32[9,4,16,256]{3,2,1,0:T(8,128)} custom-call(f32[16,3,16,128]{3,2,1,0:T(8,128)S(1)} %bitcast.10, bf16[256,768]{1,0:T(8,128)(2,1)S(1)} %copy-done.5, bf16[256,768]{1,0:T(8,128)(2,1)S(1)} %copy-done.4), custom_call_target="tpu_custom_call" | custom-call | tf_op jit(solution)/shard_map/pallas_call | solution.py:227
Async XLA Ops:
  0.0 58.4 %copy-start.2 = (bf16[2,128,1024]{2,1,0:T(8,128)(2,1)S(1)}, bf16[2,128,1024]{2,1,0:T(8,128)(2,1)}, u32[]{:S(2)}) copy-start(bf16[2,128,1024]{2,1,0:T(8,128)(2,1)} %constant.21.clone.low_ref) | copy-start | bytes 1572868
  0.0 58.4 %copy-start.3 = (bf16[2,128,1024]{2,1,0:T(8,128)(2,1)S(1)}, bf16[2,128,1024]{2,1,0:T(8,128)(2,1)}, u32[]{:S(2)}) copy-start(bf16[2,128,1024]{2,1,0:T(8,128)(2,1)} %constant.20.clone.high_ref) | copy-start | bytes 1572868
  58.4 22.8 %copy-start = (bf16[2,1024,128]{2,1,0:T(8,128)(2,1)S(1)}, bf16[2,1024,128]{2,1,0:T(8,128)(2,1)}, u32[]{:S(2)}) copy-start(bf16[2,1024,128]{2,1,0:T(8,128)(2,1)} %constant.23.clone.low_ref) | copy-start | bytes 1572868
  58.4 22.8 %copy-start.1 = (bf16[2,1024,128]{2,1,0:T(8,128)(2,1)S(1)}, bf16[2,1024,128]{2,1,0:T(8,128)(2,1)}, u32[]{:S(2)}) copy-start(bf16[2,1024,128]{2,1,0:T(8,128)(2,1)} %constant.22.clone.high_ref) | copy-start | bytes 1572868
  58.4 36.7 %copy-start.8 = (bf16[384,128]{1,0:T(8,128)(2,1)S(1)}, bf16[384,128]{1,0:T(8,128)(2,1)}, u32[]{:S(2)}) copy-start(bf16[384,128]{1,0:T(8,128)(2,1)} %constant.25.clone.low_ref) | copy-start | bytes 294916
  58.4 36.7 %copy-start.9 = (bf16[384,128]{1,0:T(8,128)(2,1)S(1)}, bf16[384,128]{1,0:T(8,128)(2,1)}, u32[]{:S(2)}) copy-start(bf16[384,128]{1,0:T(8,128)(2,1)} %constant.24.clone.high_ref) | copy-start | bytes 294916
  58.4 49.0 %copy-start.6 = (bf16[768,256]{1,0:T(8,128)(2,1)S(1)}, bf16[768,256]{1,0:T(8,128)(2,1)}, u32[]{:S(2)}) copy-start(bf16[768,256]{1,0:T(8,128)(2,1)} %constant.27.clone.low_ref) | copy-start | bytes 1179652
  58.4 49.0 %copy-start.7 = (bf16[768,256]{1,0:T(8,128)(2,1)S(1)}, bf16[768,256]{1,0:T(8,128)(2,1)}, u32[]{:S(2)}) copy-start(bf16[768,256]{1,0:T(8,128)(2,1)} %constant.26.clone.high_ref) | copy-start | bytes 1179652
  59.8 62.9 %copy-start.4 = (bf16[256,768]{1,0:T(8,128)(2,1)S(1)}, bf16[256,768]{1,0:T(8,128)(2,1)}, u32[]{:S(2)}) copy-start(bf16[256,768]{1,0:T(8,128)(2,1)} %constant.29.clone.low_ref) | copy-start | bytes 1179652
  59.8 62.9 %copy-start.5 = (bf16[256,768]{1,0:T(8,128)(2,1)S(1)}, bf16[256,768]{1,0:T(8,128)(2,1)}, u32[]{:S(2)}) copy-start(bf16[256,768]{1,0:T(8,128)(2,1)} %constant.28.clone.high_ref) | copy-start | bytes 1179652
